TPU v7x, 32 devices: a whole 2x2x4 slice. The times are simulated.
32 devices in a mesh: vox: 2 (over y), subj: 4 (over z), site: 4 (over x, core).
Axes of the slice: x: 2, y: 2, z: 4, core: 2. Of those that a mesh axis runs over, the one named last changes fastest.
Arguments:
- voxel_data: bfloat16 [2048, 8, 8, 128], P(('subj', 'site'), 'vox'), may hold values from -6 to 6
- site_label: int32 [2048], P(('subj', 'site')), may hold values from 0 to 59, as said below
- covariates: bfloat16 [2048, 40], P(('subj', 'site')), may hold values from -0.375 to 0.375
- brain_mask: int32 [8, 8, 128], P('vox'), may hold values 0 or 1
Outputs:
- cross_product: float32 [40, 8192], P(None, ('vox', 'subj', 'site'))
Inputs may be any that keep to these rules, and one draw needn't show every extreme that they name: `site_label`: every site has at least 8 subjects.
All inputs are finite; a program needn't handle non-finite values. No bound on the sum of `brain_mask` on one device may be relied on, other than what follows from the above.
Results may differ from a plain program's by a relative error of at most 0.002.
The roundings to bfloat16 on the way count: a program that leaves them out, or rounds other values in their place, can miss the bound.
Values may be sent and summed in bfloat16 or wider, within the bound.
A program may use at most 64 MiB of HBM per device.

v0:
```python
import jax
import jax.numpy as jnp
from jax import lax
from jax.sharding import PartitionSpec as P

NSITE = 60
PASSES = 3
EB_ITERS = 5


center_weight = 0.1
along_weight = 0.35
across_weight = 0.05


def with_halo(block, sides, width):
    for axis, dim in sides:
        count = lax.axis_size(axis)
        forward = [(i, i + 1) for i in range(count - 1)]
        backward = [(target, source) for source, target in forward]
        low = lax.ppermute(
            lax.slice_in_dim(block, block.shape[dim] - width, None, axis=dim), axis, forward
        )
        high = lax.ppermute(lax.slice_in_dim(block, 0, width, axis=dim), axis, backward)
        block = jnp.concatenate([low, block, high], axis=dim)
    return block


def kernel_pass(extended, mask_part):
    wide = extended.astype(jnp.float32)
    core = wide[:, 1:-1]
    along = wide[:, 2:] + wide[:, :-2]
    padded = jnp.pad(core, ((0, 0), (0, 0), (1, 1), (1, 1)))
    across = (
        padded[:, :, 2:, 1:-1]
        + padded[:, :, :-2, 1:-1]
        + padded[:, :, 1:-1, 2:]
        + padded[:, :, 1:-1, :-2]
    )
    mixed = center_weight * core + along_weight * along + across_weight * across
    return (mixed * mask_part).astype(jnp.bfloat16)


def faces_of(current):
    return with_halo(current, (("vox", 1),), 1)


def site_stats(moments, counts):
    first = moments[0]
    second = moments[1]
    total = jnp.sum(counts)
    voxel_mean = jnp.sum(first, axis=0) / total
    voxel_var = jnp.sum(second, axis=0) / total - voxel_mean * voxel_mean + 1e-05
    column = counts[:, None]
    sum_z = (first - column * voxel_mean) / jnp.sqrt(voxel_var)
    sum_zz = (second - 2.0 * voxel_mean * first + column * voxel_mean * voxel_mean) / voxel_var
    gamma_hat = sum_z / column
    delta_hat = (sum_zz - sum_z * sum_z / column) / (column - 1.0)
    return (voxel_mean, voxel_var, sum_z, sum_zz, gamma_hat, delta_hat)


def prior_terms(gamma_hat, delta_hat, weights):
    terms = jnp.stack(
        [
            jnp.sum(weights * gamma_hat, axis=1),
            jnp.sum(weights * gamma_hat * gamma_hat, axis=1),
            jnp.sum(weights * delta_hat, axis=1),
            jnp.sum(weights * delta_hat * delta_hat, axis=1),
        ]
    )
    return (terms, jnp.sum(weights))


def eb_tables(terms, weight_total, counts, voxel_var, sum_z, sum_zz, gamma_hat, delta_hat):
    gamma_bar = (terms[0] / weight_total)[:, None]
    tau_sq = (terms[1] / weight_total)[:, None] - gamma_bar * gamma_bar + 1e-06
    delta_mean = (terms[2] / weight_total)[:, None]
    delta_var = (terms[3] / weight_total)[:, None] - delta_mean * delta_mean + 1e-06
    shape_a = (2.0 * delta_var + delta_mean * delta_mean) / delta_var
    shape_b = (delta_mean * delta_var + delta_mean * delta_mean * delta_mean) / delta_var
    column = counts[:, None]
    gamma_star = gamma_hat
    delta_star = delta_hat
    for step in range(EB_ITERS):
        gamma_star = (column * tau_sq * gamma_hat + delta_star * gamma_bar) / (
            column * tau_sq + delta_star
        )
        spread = sum_zz - 2.0 * gamma_star * sum_z + column * gamma_star * gamma_star
        delta_star = (shape_b + 0.5 * spread) / (0.5 * column + shape_a - 1.0)
    shift = (jnp.sqrt(voxel_var) * gamma_star).astype(jnp.bfloat16)
    scale = (1.0 / jnp.sqrt(delta_star)).astype(jnp.bfloat16)
    return (shift, scale)


def per_device(voxel_data, site_label, covariates, brain_mask):
    rows = voxel_data.shape[0]
    tile_cells = voxel_data.shape[1] * voxel_data.shape[2] * voxel_data.shape[3]
    mask_float = brain_mask.astype(jnp.float32)
    current = voxel_data
    for step in range(PASSES):
        current = kernel_pass(faces_of(current), mask_float)
    smoothed = current.reshape(rows, tile_cells)
    sites = jnp.arange(NSITE, dtype=jnp.int32)
    onehot = (site_label[:, None] == sites[None, :]).astype(jnp.bfloat16)
    wide = smoothed.astype(jnp.float32)
    square = (wide * wide).astype(jnp.bfloat16)
    first = jnp.dot(onehot.T, smoothed, preferred_element_type=jnp.float32)
    second = jnp.dot(onehot.T, square, preferred_element_type=jnp.float32)
    moments = jnp.stack([first, second])
    counts = jnp.sum(onehot.astype(jnp.float32), axis=0)
    weights = mask_float.reshape(tile_cells)
    moments, counts = lax.psum((moments, counts), ("subj", "site"))
    voxel_mean, voxel_var, sum_z, sum_zz, gamma_hat, delta_hat = site_stats(moments, counts)
    local_terms, local_weight = prior_terms(gamma_hat, delta_hat, weights)
    terms, weight_total = lax.psum((local_terms, local_weight), "vox")
    shift, scale = eb_tables(
        terms, weight_total, counts, voxel_var, sum_z, sum_zz, gamma_hat, delta_hat
    )
    shift_at = jnp.dot(onehot, shift, preferred_element_type=jnp.float32)
    scale_at = jnp.dot(onehot, scale, preferred_element_type=jnp.float32)
    adjusted = ((wide - voxel_mean - shift_at) * scale_at + voxel_mean).astype(jnp.bfloat16)
    partial_value = jnp.dot(covariates.T, adjusted, preferred_element_type=jnp.float32)
    summed = lax.psum(partial_value, ("subj", "site"))
    piece = tile_cells // lax.axis_size(("subj", "site"))
    return lax.dynamic_slice_in_dim(summed, lax.axis_index(("subj", "site")) * piece, piece, 1)


def solution(mesh):
    in_specs = (
        P(("subj", "site"), "vox", None, None),
        P(("subj", "site")),
        P(("subj", "site"), None),
        P("vox", None, None),
    )
    out_specs = P(None, ("vox", "subj", "site"))
    return jax.shard_map(
        per_device, mesh=mesh, in_specs=in_specs, out_specs=out_specs, check_vma=False
    )
```

profile of v0, /device:TPU:0, one launch (start us, length us, event | category | flops | bytes accessed | tf_op | source)
XLA Modules:
  0.0 271.6 jit_solution(15357779289124389344)
XLA Ops:
  7.6 4.9 %collective-permute-start = (bf16[128,1,8,128]{3,2,1,0:T(8,128)(2,1)S(1)}, bf16[128,1,8,128]{3,2,1,0:T(8,128)(2,1)S(1)}, u32[]{:S(2)}, u32[]{:S(2)}) collective-permute-start(bf16[128,1,8,128]{3,2,1,0:T(8,128)(2,1)S(1)} %get-tuple-element.30), channel_id=1, source_target_pairs={{0,16},{1,17},{2,18},{3,19},{4,20},{5,21},{6,22},{7,23},{8,24},{9,... | collective-permute-start | bytes 786440 | tf_op jit(solution)/shard_map/ppermute | solution.py:21
  14.5 3.5 %collective-permute-done = bf16[128,1,8,128]{3,2,1,0:T(8,128)(2,1)S(1)} collective-permute-done((bf16[128,1,8,128]{3,2,1,0:T(8,128)(2,1)S(1)}, bf16[128,1,8,128]{3,2,1,0:T(8,128)(2,1)S(1)}, u32[]{:S(2)}, u32[]{:S(2)}) %collective-permute-start) | collective-permute-done | bytes 262176 | tf_op jit(solution)/shard_map/ppermute | solution.py:21
  18.1 4.1 %collective-permute-done.1 = bf16[128,1,8,128]{3,2,1,0:T(8,128)(2,1)S(1)} collective-permute-done((bf16[128,1,8,128]{3,2,1,0:T(8,128)(2,1)S(1)}, bf16[128,1,8,128]{3,2,1,0:T(8,128)(2,1)S(1)}, u32[]{:S(2)}, u32[]{:S(2)}) %collective-permute-start.1) | collective-permute-done | bytes 262176 | tf_op jit(solution)/shard_map/ppermute | solution.py:24
  22.2 1.6 maximum_convert_fusion
  24.0 1.5 fusion.9
  25.5 1.5 collective-permute-start.2
  28.3 3.2 %collective-permute-done.2 = bf16[128,1,8,128]{3,2,1,0:T(8,128)(2,1)S(1)} collective-permute-done((bf16[128,1,8,128]{3,2,1,0:T(8,128)(2,1)S(1)}, bf16[128,1,8,128]{3,2,1,0:T(8,128)(2,1)S(1)}, u32[]{:S(2)}, u32[]{:S(2)}) %collective-permute-start.2) | collective-permute-done | bytes 262176 | tf_op jit(solution)/shard_map/ppermute | solution.py:21
  31.5 4.1 %collective-permute-done.3 = bf16[128,1,8,128]{3,2,1,0:T(8,128)(2,1)S(1)} collective-permute-done((bf16[128,1,8,128]{3,2,1,0:T(8,128)(2,1)S(1)}, bf16[128,1,8,128]{3,2,1,0:T(8,128)(2,1)S(1)}, u32[]{:S(2)}, u32[]{:S(2)}) %collective-permute-start.3) | collective-permute-done | bytes 262176 | tf_op jit(solution)/shard_map/ppermute | solution.py:24
  36.2 1.5 fusion.16
  37.7 1.5 collective-permute-start.4
  40.5 2.6 collective-permute-done.4
  43.0 4.4 %collective-permute-done.5 = bf16[128,1,8,128]{3,2,1,0:T(8,128)(2,1)S(1)} collective-permute-done((bf16[128,1,8,128]{3,2,1,0:T(8,128)(2,1)S(1)}, bf16[128,1,8,128]{3,2,1,0:T(8,128)(2,1)S(1)}, u32[]{:S(2)}, u32[]{:S(2)}) %collective-permute-start.5) | collective-permute-done | bytes 262176 | tf_op jit(solution)/shard_map/ppermute | solution.py:24
  48.1 1.5 fusion.23
  50.5 1.4 pad_maximum_fusion
  52.1 30.5 %psum.36 = f32[60]{0:T(128)S(1)} all-reduce(f32[60]{0:T(128)S(1)} %convert_reduce_fusion), channel_id=1, replica_groups=mesh['vox'=2,'subj'=4,'site'=4] {'subj','site'}, use_global_device_ids=true, to_apply=%region_3.4 | all-reduce | flops 60 | bytes 480 | tf_op jit(solution)/shard_map/psum | solution.py:112
  83.8 66.6 %all-reduce.7.cloned.1.call-done = f32[2,60,4096]{2,1,0:T(8,128)} async-done(((f32[2,60,4096]{2,1,0:T(8,128)}), f32[2,60,4096]{2,1,0:T(8,128)}) %all-reduce.7.cloned.1.call-update) | async-done | bytes 1966096 | tf_op jit(solution)/shard_map/psum | solution.py:112
  150.4 1.8 slice_reduce_fusion
  153.0 2.6 multiply_reduce_fusion.1
  155.6 5.6 %all-reduce.3 = (f32[4,60]{1,0:T(4,128)S(1)}, f32[]{:T(128)}) all-reduce(f32[4,60]{1,0:T(4,128)S(1)} %pad_maximum_fusion.1, f32[]{:T(128)} %convert_reduce_fusion.1), channel_id=1, replica_groups=mesh['vox'=2,'subj'=4,'site'=4] {'vox'}, use_global_device_ids=true, to_apply=%region_10.11 | all-reduce | flops 241 | bytes 1928 | tf_op jit(solution)/shard_map/psum | solution.py:115
  161.9 3.8 %add_divide_fusion = f32[60,4096]{1,0:T(8,128)S(1)} fusion(f32[60,4096]{1,0:T(8,128)} %get-tuple-element.22, f32[60,4096]{1,0:T(8,128)} %get-tuple-element.21, f32[60,4096]{1,0:T(8,128)} %get-tuple-element.20, f32[60]{0:T(128)S(1)} %add_add_fusion, f32[60]{0:T(128)S(1)} %get-tuple-element.16, f32[60]{0:T(128)S(1)} %get-tuple-element.34, ...), kind=kLoop, calls=%fused_computation.97 | loop fusion | flops 14745600 | bytes 4949168 | tf_op jit(solution)/shard_map/div | solution.py:85
  166.7 2.0 convolution_subtract_fusion
  168.7 4.2 %convolution_bitcast_fusion.2 = f32[40,4096]{1,0:T(8,128)} fusion(bf16[128,40]{0,1:T(8,128)(2,1)S(1)} %copy-done, f32[128,4096]{1,0:T(8,128)} %convolution_subtract_fusion, f32[4096]{0:T(1024)S(1)} %get-tuple-element.25, f32[60,4096]{1,0:T(8,128)} %copy-done.2, f32[60,4096]{1,0:T(8,128)} %get-tuple-element.22, f32[60]{0:T(128)S(1)} %add_add_fusion, ...), kind=kOutput, calls=%fused_computation.18 | convolution fusion | flops 109633024 | bytes 5828608 | tf_op jit(solution)/shard_map/dot_general | solution.py:122
  172.9 90.4 %all-reduce.9.cloned.1.call-done = f32[40,4096]{1,0:T(8,128)} async-done(((f32[40,4096]{1,0:T(8,128)}), f32[40,4096]{1,0:T(8,128)}) %all-reduce.9.cloned.1.call-update) | async-done | bytes 655376 | tf_op jit(solution)/shard_map/psum | solution.py:123
  263.3 1.4 constant_dynamic-slice_fusion
  (36 shorter events, 11.9 us)
Async XLA Ops:
  6.5 162.2 %copy-start = (bf16[128,40]{0,1:T(8,128)(2,1)S(1)}, bf16[128,40]{0,1:T(8,128)(2,1)}, u32[]{:S(2)}) copy-start(bf16[128,40]{0,1:T(8,128)(2,1)} %param.6) | copy-start | bytes 30724
  6.5 143.9 %all-reduce.7.cloned.1.call-start = ((), (), s32[]{:S(2)}) async-start(), calls=%async_computation | async-start | bytes 4194304 | tf_op jit(solution)/shard_map/psum | solution.py:112
  7.6 10.4 %collective-permute-start = (bf16[128,1,8,128]{3,2,1,0:T(8,128)(2,1)S(1)}, bf16[128,1,8,128]{3,2,1,0:T(8,128)(2,1)S(1)}, u32[]{:S(2)}, u32[]{:S(2)}) collective-permute-start(bf16[128,1,8,128]{3,2,1,0:T(8,128)(2,1)S(1)} %get-tuple-element.30), channel_id=1, source_target_pairs={{0,16},{1,17},{2,18},{3,19},{4,20},{5,21},{6,22},{7,23},{8,24},{9,... | collective-permute-start | bytes 786440 | tf_op jit(solution)/shard_map/ppermute | solution.py:21
  12.5 9.7 %collective-permute-start.1 = (bf16[128,1,8,128]{3,2,1,0:T(8,128)(2,1)S(1)}, bf16[128,1,8,128]{3,2,1,0:T(8,128)(2,1)S(1)}, u32[]{:S(2)}, u32[]{:S(2)}) collective-permute-start(bf16[128,1,8,128]{3,2,1,0:T(8,128)(2,1)S(1)} %get-tuple-element.31), channel_id=1, source_target_pairs={{16,0},{17,1},{18,2},{19,3},{20,4},{21,5},{22,6},{23,7},{24,8},{25... | collective-permute-start | bytes 786440 | tf_op jit(solution)/shard_map/ppermute | solution.py:24
  25.5 5.9 %collective-permute-start.2 = (bf16[128,1,8,128]{3,2,1,0:T(8,128)(2,1)S(1)}, bf16[128,1,8,128]{3,2,1,0:T(8,128)(2,1)S(1)}, u32[]{:S(2)}, u32[]{:S(2)}) collective-permute-start(bf16[128,1,8,128]{3,2,1,0:T(8,128)(2,1)S(1)} %get-tuple-element.28), channel_id=1, source_target_pairs={{0,16},{1,17},{2,18},{3,19},{4,20},{5,21},{6,22},{7,23},{8,24},{9,... | collective-permute-start | bytes 786440 | tf_op jit(solution)/shard_map/ppermute | solution.py:21
  27.0 8.6 %collective-permute-start.3 = (bf16[128,1,8,128]{3,2,1,0:T(8,128)(2,1)S(1)}, bf16[128,1,8,128]{3,2,1,0:T(8,128)(2,1)S(1)}, u32[]{:S(2)}, u32[]{:S(2)}) collective-permute-start(bf16[128,1,8,128]{3,2,1,0:T(8,128)(2,1)S(1)} %get-tuple-element.29), channel_id=1, source_target_pairs={{16,0},{17,1},{18,2},{19,3},{20,4},{21,5},{22,6},{23,7},{24,8},{25... | collective-permute-start | bytes 786440 | tf_op jit(solution)/shard_map/ppermute | solution.py:24
  37.7 5.3 %collective-permute-start.4 = (bf16[128,1,8,128]{3,2,1,0:T(8,128)(2,1)S(1)}, bf16[128,1,8,128]{3,2,1,0:T(8,128)(2,1)S(1)}, u32[]{:S(2)}, u32[]{:S(2)}) collective-permute-start(bf16[128,1,8,128]{3,2,1,0:T(8,128)(2,1)S(1)} %get-tuple-element.26), channel_id=1, source_target_pairs={{0,16},{1,17},{2,18},{3,19},{4,20},{5,21},{6,22},{7,23},{8,24},{9,... | collective-permute-start | bytes 786440 | tf_op jit(solution)/shard_map/ppermute | solution.py:21
  39.2 8.3 %collective-permute-start.5 = (bf16[128,1,8,128]{3,2,1,0:T(8,128)(2,1)S(1)}, bf16[128,1,8,128]{3,2,1,0:T(8,128)(2,1)S(1)}, u32[]{:S(2)}, u32[]{:S(2)}) collective-permute-start(bf16[128,1,8,128]{3,2,1,0:T(8,128)(2,1)S(1)} %get-tuple-element.27), channel_id=1, source_target_pairs={{16,0},{17,1},{18,2},{19,3},{20,4},{21,5},{22,6},{23,7},{24,8},{25... | collective-permute-start | bytes 786440 | tf_op jit(solution)/shard_map/ppermute | solution.py:24
  48.0 1.5 copy-start.4
  51.9 30.7 %copy-start.3 = (s32[4,8,128]{2,1,0:T(8,128)S(1)}, s32[4,8,128]{2,1,0:T(8,128)}, u32[]{:S(2)}) copy-start(s32[4,8,128]{2,1,0:T(8,128)} %param.7) | copy-start | bytes 49156
  52.0 211.4 %all-reduce.9.cloned.1.call-start = ((), (), s32[]{:S(2)}) async-start(), calls=%async_computation.1 | async-start | bytes 1310720 | tf_op jit(solution)/shard_map/psum | solution.py:123
  150.4 2.5 copy-start.1
  165.7 1.0 copy-start.2
Sparse Core Ops, SparseCore 0:
  52.1 98.3 all-reduce.6
  173.0 90.2 all-reduce.8
where the time goes:
time: 272 us
  waiting for transfers between devices  179 us (66%)
  blocking collectives  36.1 us (13%)
  other arithmetic  19.7 us (7%)
  between operations  13.6 us (5%)
  starting transfers between devices  11.7 us (4%)
  matrix products  7.13 us (3%)
  local copies, waits for them, and re-layouts  4.3 us (2%)
    psum x1, waiting for transfers between devices, per_device(): summed = lax.psum(partial_value, ('subj', 'site'))  90.4 us
    psum x1, waiting for transfers between devices, per_device(): moments, counts = lax.psum((moments, counts), ('subj', 'site'))  66.6 us
    psum x1, blocking collectives, per_device(): moments, counts = lax.psum((moments, counts), ('subj', 'site'))  30.5 us
    ppermute x3, waiting for transfers between devices, with_halo(): lax.ppermute(lax.slice_in_dim(block, 0, width, axis=dim), axis, backward)  12.7 us
    ppermute x3, waiting for transfers between devices, with_halo(): lax.ppermute(lax.slice_in_dim(block, block.shape[dim] - width, None, axis...  9.23 us
    ppermute x3, starting transfers between devices, with_halo(): lax.ppermute(lax.slice_in_dim(block, block.shape[dim] - width, None, axis...  7.82 us
    psum x1, blocking collectives, per_device(): terms, weight_total = lax.psum((local_terms, local_weight), 'vox')  5.63 us
  transfers between devices with their start and end apart: 8, of which 8 were waited for; matrix products, arithmetic and copies ran while one was open for 1% of the time, Pallas kernels for 0%

commit v1 on v0

--- a/solution.py
+++ b/solution.py
@@ -13,19 +13,6 @@
 across_weight = 0.05
 
 
-def with_halo(block, sides, width):
-    for axis, dim in sides:
-        count = lax.axis_size(axis)
-        forward = [(i, i + 1) for i in range(count - 1)]
-        backward = [(target, source) for source, target in forward]
-        low = lax.ppermute(
-            lax.slice_in_dim(block, block.shape[dim] - width, None, axis=dim), axis, forward
-        )
-        high = lax.ppermute(lax.slice_in_dim(block, 0, width, axis=dim), axis, backward)
-        block = jnp.concatenate([low, block, high], axis=dim)
-    return block
-
-
 def kernel_pass(extended, mask_part):
     wide = extended.astype(jnp.float32)
     core = wide[:, 1:-1]
@@ -38,11 +25,7 @@
         + padded[:, :, 1:-1, :-2]
     )
     mixed = center_weight * core + along_weight * along + across_weight * across
-    return (mixed * mask_part).astype(jnp.bfloat16)
-
-
-def faces_of(current):
-    return with_halo(current, (("vox", 1),), 1)
+    return lax.reduce_precision(mixed * mask_part, 8, 7).astype(jnp.bfloat16)
 
 
 def site_stats(moments, counts):
@@ -92,37 +75,51 @@
     return (shift, scale)
 
 
+def widen(block, width):
+    count = lax.axis_size("vox")
+    forward = [(i, i + 1) for i in range(count - 1)]
+    backward = [(target, source) for source, target in forward]
+    low = lax.ppermute(lax.slice_in_dim(block, block.shape[1] - width, None, axis=1), "vox", forward)
+    high = lax.ppermute(lax.slice_in_dim(block, 0, width, axis=1), "vox", backward)
+    return jnp.concatenate([low, block, high], axis=1)
+
+
 def per_device(voxel_data, site_label, covariates, brain_mask):
+    group = ("subj", "site")
     rows = voxel_data.shape[0]
     tile_cells = voxel_data.shape[1] * voxel_data.shape[2] * voxel_data.shape[3]
-    mask_float = brain_mask.astype(jnp.float32)
-    current = voxel_data
+    members = lax.axis_size(group)
+    piece = tile_cells // members
+    me = lax.axis_index(group)
+    labels = lax.all_gather(site_label, group, tiled=True)
+    covs = lax.all_gather(covariates, group, tiled=True)
+    masks = widen(brain_mask.astype(jnp.bfloat16)[None], PASSES)[0].astype(jnp.float32)
+    current = widen(voxel_data, PASSES)
     for step in range(PASSES):
-        current = kernel_pass(faces_of(current), mask_float)
-    smoothed = current.reshape(rows, tile_cells)
+        masks = masks[1:-1]
+        current = kernel_pass(current, masks)
+    smoothed = current.reshape(rows, members, piece)
+    smoothed = lax.all_to_all(smoothed, group, 1, 0, tiled=True).reshape(rows * members, piece)
     sites = jnp.arange(NSITE, dtype=jnp.int32)
-    onehot = (site_label[:, None] == sites[None, :]).astype(jnp.bfloat16)
+    onehot = (labels[:, None] == sites[None, :]).astype(jnp.bfloat16)
     wide = smoothed.astype(jnp.float32)
     square = (wide * wide).astype(jnp.bfloat16)
     first = jnp.dot(onehot.T, smoothed, preferred_element_type=jnp.float32)
     second = jnp.dot(onehot.T, square, preferred_element_type=jnp.float32)
-    moments = jnp.stack([first, second])
     counts = jnp.sum(onehot.astype(jnp.float32), axis=0)
-    weights = mask_float.reshape(tile_cells)
-    moments, counts = lax.psum((moments, counts), ("subj", "site"))
-    voxel_mean, voxel_var, sum_z, sum_zz, gamma_hat, delta_hat = site_stats(moments, counts)
+    weights = lax.dynamic_slice_in_dim(brain_mask.reshape(tile_cells), me * piece, piece, 0).astype(jnp.float32)
+    stats = site_stats((first, second), counts)
+    voxel_mean, voxel_var, sum_z, sum_zz, gamma_hat, delta_hat = stats
     local_terms, local_weight = prior_terms(gamma_hat, delta_hat, weights)
-    terms, weight_total = lax.psum((local_terms, local_weight), "vox")
+    packed = jnp.concatenate([local_terms, jnp.full((1, NSITE), local_weight)])
+    packed = lax.psum(packed, ("vox", "subj", "site"))
     shift, scale = eb_tables(
-        terms, weight_total, counts, voxel_var, sum_z, sum_zz, gamma_hat, delta_hat
+        packed[:4], packed[4, 0], counts, voxel_var, sum_z, sum_zz, gamma_hat, delta_hat
     )
     shift_at = jnp.dot(onehot, shift, preferred_element_type=jnp.float32)
     scale_at = jnp.dot(onehot, scale, preferred_element_type=jnp.float32)
     adjusted = ((wide - voxel_mean - shift_at) * scale_at + voxel_mean).astype(jnp.bfloat16)
-    partial_value = jnp.dot(covariates.T, adjusted, preferred_element_type=jnp.float32)
-    summed = lax.psum(partial_value, ("subj", "site"))
-    piece = tile_cells // lax.axis_size(("subj", "site"))
-    return lax.dynamic_slice_in_dim(summed, lax.axis_index(("subj", "site")) * piece, piece, 1)
+    return jnp.dot(covs.T, adjusted, preferred_element_type=jnp.float32)
 
 
 def solution(mesh):

time: 272 us -> 152 us (0.56)
  waiting for transfers between devices: 179 us -> 19 us
  blocking collectives: 36.1 us -> 92.2 us
  between operations: 13.6 us -> 0.24 us
  other arithmetic: 19.7 us -> 13 us
  starting transfers between devices: 11.7 us -> 17.9 us
  matrix products: 7.13 us -> 3.01 us
    psum x2 -> x0, waiting for transfers between devices: 157 us -> none  [the longest x1 90.4 us: per_device(): summed = lax.psum(partial_value, ('subj', 'site'))]
    all_gather x0 -> x2, blocking collectives: none -> 55.3 us  [the longest x1 33.3 us: per_device(): labels = lax.all_gather(site_label, group, tiled=True)]
    all_to_all x0 -> x1, starting transfers between devices: none -> 5.91 us  [per_device(): lax.all_to_all(smoothed, group, 1, 0, tiled=True)]
    reduce_sum x2 -> x1, other arithmetic: 4.44 us -> 0.25 us  [prior_terms(): jnp.sum(weights * delta_hat * delta_hat, axis=1)]
    div x1 -> x0, other arithmetic: 3.82 us -> none  [eb_tables(): (column * tau_sq * gamma_hat + delta_star * gamma_bar) / (column * tau_sq...]
    convert_element_type x3, other arithmetic: 2.26 us -> 5.53 us  [kernel_pass(): wide = extended.astype(jnp.float32)]
    ppermute x6 -> x4, waiting for transfers between devices: 21.9 us -> 19 us  [the longest x2 14.8 us: widen(): lax.ppermute(lax.slice_in_dim(block, block.shape[1] - width, None, axis=1...]
    psum x2 -> x1, blocking collectives: 36.1 us -> 36.9 us  [per_device(): packed = lax.psum(packed, ('vox', 'subj', 'site'))]
  transfers between devices with their start and end apart: 8 -> 5, of which waited for: 8 -> 2; matrix products, arithmetic and copies ran while one was open for 1% -> 3% of each run, Pallas kernels for 0% -> 0%
where the time goes in v1:
time: 152 us; the launch traced here: 150 us
  blocking collectives  92.2 us (61%)
  waiting for transfers between devices  19 us (12%)
  starting transfers between devices  17.9 us (12%)
  other arithmetic  13 us (9%)
  local copies, waits for them, and re-layouts  4.94 us (3%)
  matrix products  3.01 us (2%)
    psum x1, blocking collectives, per_device(): packed = lax.psum(packed, ('vox', 'subj', 'site'))  36.9 us
    all_gather x1, blocking collectives, per_device(): labels = lax.all_gather(site_label, group, tiled=True)  33.3 us
    all_gather x1, blocking collectives, per_device(): covs = lax.all_gather(covariates, group, tiled=True)  22 us
    ppermute x2, waiting for transfers between devices, widen(): lax.ppermute(lax.slice_in_dim(block, block.shape[1] - width, None, axis=1...  14.8 us
    ppermute x2, starting transfers between devices, widen(): lax.ppermute(lax.slice_in_dim(block, block.shape[1] - width, None, axis=1...  9.45 us
    all_to_all x1, starting transfers between devices, per_device(): lax.all_to_all(smoothed, group, 1, 0, tiled=True)  5.91 us
    convert_element_type x3, other arithmetic, kernel_pass(): wide = extended.astype(jnp.float32)  5.53 us
    ppermute x2, waiting for transfers between devices, widen(): lax.ppermute(lax.slice_in_dim(block, 0, width, axis=1), 'vox', backward)  4.16 us
  transfers between devices with their start and end apart: 5, of which 2 were waited for; matrix products, arithmetic and copies ran while one was open for 3% of the time, Pallas kernels for 0%

profile of v1, /device:TPU:0, one launch (start us, length us, event | category | flops | bytes accessed | tf_op | source)
XLA Modules:
  0.0 150.3 jit_solution(16454163508243912495)
XLA Ops:
  0.0 0.7 convert_bitcast_fusion
  0.7 4.9 %collective-permute-start.2 = (bf16[1,3,8,128]{3,2,1,0:T(8,128)(2,1)S(1)}, bf16[1,3,8,128]{3,2,1,0:T(8,128)(2,1)S(1)}, u32[]{:S(2)}, u32[]{:S(2)}) collective-permute-start(bf16[1,3,8,128]{3,2,1,0:T(8,128)(2,1)S(1)} %get-tuple-element.28), channel_id=1, source_target_pairs={{0,16},{1,17},{2,18},{3,19},{4,20},{5,21},{6,22},{7,23},{8,24},{9,... | collective-permute-start | bytes 18440 | tf_op jit(solution)/shard_map/ppermute | solution.py:82
  5.6 1.3 collective-permute-start.3
  6.9 2.0 %copy.13 = bf16[128,4,8,128]{0,3,2,1:T(8,128)(2,1)S(1)} copy(bf16[128,4,8,128]{3,2,1,0:T(8,128)(2,1)} %param.4) | data formatting | bytes 2097152 | tf_op args[0]
  9.2 4.6 %collective-permute-start = (bf16[128,3,8,128]{0,3,2,1:T(8,128)(2,1)S(1)}, bf16[128,3,8,128]{0,3,2,1:T(8,128)(2,1)S(1)}, u32[]{:S(2)}, u32[]{:S(2)}) collective-permute-start(bf16[128,3,8,128]{0,3,2,1:T(8,128)(2,1)S(1)} %get-tuple-element.26), channel_id=1, source_target_pairs={{0,16},{1,17},{2,18},{3,19},{4,20},{5,21},{6,22},{7,23},{8,24},{9,... | collective-permute-start | bytes 2359304 | tf_op jit(solution)/shard_map/ppermute | solution.py:82
  13.8 1.3 collective-permute-start.1
  15.1 14.8 %collective-permute-done = bf16[128,3,8,128]{0,3,2,1:T(8,128)(2,1)S(1)} collective-permute-done((bf16[128,3,8,128]{0,3,2,1:T(8,128)(2,1)S(1)}, bf16[128,3,8,128]{0,3,2,1:T(8,128)(2,1)S(1)}, u32[]{:S(2)}, u32[]{:S(2)}) %collective-permute-start) | collective-permute-done | bytes 786464 | tf_op jit(solution)/shard_map/ppermute | solution.py:82
  29.9 4.2 %collective-permute-done.1 = bf16[128,3,8,128]{0,3,2,1:T(8,128)(2,1)S(1)} collective-permute-done((bf16[128,3,8,128]{0,3,2,1:T(8,128)(2,1)S(1)}, bf16[128,3,8,128]{0,3,2,1:T(8,128)(2,1)S(1)}, u32[]{:S(2)}, u32[]{:S(2)}) %collective-permute-start.1) | collective-permute-done | bytes 786464 | tf_op jit(solution)/shard_map/ppermute | solution.py:83
  35.0 2.9 %fusion.33 = f32[128,8,8,128]{0,3,2,1:T(8,128)S(1)} fusion(f32[8,8,128]{2,1,0:T(8,128)S(1)} %slice_bitcast_fusion, f32[128,8,8,128]{0,3,2,1:T(8,128)S(1)} %slice.153, f32[128,10,8,128]{0,3,2,1:T(8,128)S(1)} %maximum_convert_fusion), kind=kLoop, calls=%fused_computation.53 | loop fusion | flops 13631488 | bytes 16809984 | tf_op jit(solution)/shard_map/convert_element_type | solution.py:17
  38.1 2.2 %fusion.34 = f32[128,6,8,128]{0,3,2,1:T(8,128)S(1)} fusion(f32[6,8,128]{2,1,0:T(8,128)S(1)} %slice_bitcast_fusion.1, f32[128,6,8,128]{0,3,2,1:T(8,128)S(1)} %slice.159, f32[128,8,8,128]{0,3,2,1:T(8,128)S(1)} %fusion.33), kind=kLoop, calls=%fused_computation.54 | loop fusion | flops 10223616 | bytes 12607488 | tf_op jit(solution)/shard_map/convert_element_type | solution.py:17
  40.6 2.3 %fusion.30 = bf16[128,4,8,128]{0,3,2,1:T(8,128)(2,1)} fusion(f32[128,4,8,128]{0,3,2,1:T(8,128)S(1)} %slice.163, f32[128,6,8,128]{0,3,2,1:T(8,128)S(1)} %fusion.34, f32[4,8,128]{2,1,0:T(8,128)S(1)} %slice_bitcast_fusion.2), kind=kLoop, calls=%fused_computation.49 | loop fusion | flops 6291456 | bytes 7356416 | tf_op jit(solution)/shard_map/convert_element_type | solution.py:28
  42.9 5.9 %all-to-all-start = ((bf16[128,16,256]{0,2,1:T(8,128)(2,1)}), bf16[128,16,256]{0,2,1:T(8,128)(2,1)S(1)}, u32[]{:S(2)}, u32[]{:S(2)}) async-start(bf16[128,16,256]{0,2,1:T(8,128)(2,1)} %bitcast.4), calls=%async_computation | async-start | bytes 2097152 | tf_op jit(solution)/shard_map/all_to_all | solution.py:102
  48.8 33.3 %all-gather = s32[16,1,128]{2,1,0:T(1,128)S(1)} all-gather(s32[1,1,128]{2,1,0:T(1,128)S(1)} %bitcast.65), channel_id=1, replica_groups=mesh['vox'=2,'subj'=4,'site'=4] {'subj','site'}, dimensions={0}, use_global_device_ids=true | all-gather | bytes 8704 | tf_op jit(solution)/shard_map/all_gather | solution.py:94
  82.2 22.0 %all_gather.7 = bf16[2048,40]{0,1:T(8,128)(2,1)S(1)} all-gather(bf16[128,40]{0,1:T(8,128)(2,1)S(1)} %copy-done), channel_id=1, replica_groups=mesh['vox'=2,'subj'=4,'site'=4] {'subj','site'}, dimensions={0}, use_global_device_ids=true | all-gather | bytes 174080 | tf_op jit(solution)/shard_map/all_gather | solution.py:95
  104.1 1.4 fusion.99
  105.6 0.8 convert_reduce_fusion
  106.4 0.5 copy.16
  107.6 0.7 broadcast_multiply_fusion
  108.2 0.7 fusion.101
  109.1 0.7 broadcast_in_dim.5
  109.9 36.9 %psum.7 = f32[5,60]{1,0:T(8,128)S(1)} all-reduce(f32[5,60]{1,0:T(8,128)S(1)} %concatenate.11), channel_id=1, replica_groups=mesh['vox'=2,'subj'=4,'site'=4] {'vox','subj','site'}, use_global_device_ids=true, to_apply=%region_9.10 | all-reduce | flops 300 | bytes 2400 | tf_op jit(solution)/shard_map/psum | solution.py:115
  147.3 0.7 fusion.91
  148.0 0.7 convolution_subtract_fusion
  148.7 1.7 %fusion.36 = f32[40,256]{1,0:T(8,128)} fusion(bf16[2048,40]{0,1:T(8,128)(2,1)S(1)} %all_gather.7, f32[2048,256]{1,0:T(8,128)S(1)} %convolution_subtract_fusion, f32[256]{0:T(256)S(1)} %get-tuple-element.23, s32[2048]{0:T(1024)S(1)} %bitcast.59, f32[60,256]{1,0:T(8,128)S(1)} %get-tuple-element.21, f32[60]{0:T(128)S(1)} %add_add_fusion, ...), kind=kOutput, calls=%fused_computation.56 | convolution fusion | flops 107659264 | bytes 2497712 | tf_op jit(solution)/shard_map/dot_general | solution.py:122
  (24 shorter events, 3.1 us)
Async XLA Ops:
  0.7 14.3 %collective-permute-start.2 = (bf16[1,3,8,128]{3,2,1,0:T(8,128)(2,1)S(1)}, bf16[1,3,8,128]{3,2,1,0:T(8,128)(2,1)S(1)}, u32[]{:S(2)}, u32[]{:S(2)}) collective-permute-start(bf16[1,3,8,128]{3,2,1,0:T(8,128)(2,1)S(1)} %get-tuple-element.28), channel_id=1, source_target_pairs={{0,16},{1,17},{2,18},{3,19},{4,20},{5,21},{6,22},{7,23},{8,24},{9,... | collective-permute-start | bytes 18440 | tf_op jit(solution)/shard_map/ppermute | solution.py:82
  5.6 9.5 %collective-permute-start.3 = (bf16[1,3,8,128]{3,2,1,0:T(8,128)(2,1)S(1)}, bf16[1,3,8,128]{3,2,1,0:T(8,128)(2,1)S(1)}, u32[]{:S(2)}, u32[]{:S(2)}) collective-permute-start(bf16[1,3,8,128]{3,2,1,0:T(8,128)(2,1)S(1)} %get-tuple-element.29), channel_id=1, source_target_pairs={{16,0},{17,1},{18,2},{19,3},{20,4},{21,5},{22,6},{23,7},{24,8},{25... | collective-permute-start | bytes 18440 | tf_op jit(solution)/shard_map/ppermute | solution.py:83
  9.2 20.8 %collective-permute-start = (bf16[128,3,8,128]{0,3,2,1:T(8,128)(2,1)S(1)}, bf16[128,3,8,128]{0,3,2,1:T(8,128)(2,1)S(1)}, u32[]{:S(2)}, u32[]{:S(2)}) collective-permute-start(bf16[128,3,8,128]{0,3,2,1:T(8,128)(2,1)S(1)} %get-tuple-element.26), channel_id=1, source_target_pairs={{0,16},{1,17},{2,18},{3,19},{4,20},{5,21},{6,22},{7,23},{8,24},{9,... | collective-permute-start | bytes 2359304 | tf_op jit(solution)/shard_map/ppermute | solution.py:82
  13.8 20.3 %collective-permute-start.1 = (bf16[128,3,8,128]{0,3,2,1:T(8,128)(2,1)S(1)}, bf16[128,3,8,128]{0,3,2,1:T(8,128)(2,1)S(1)}, u32[]{:S(2)}, u32[]{:S(2)}) collective-permute-start(bf16[128,3,8,128]{0,3,2,1:T(8,128)(2,1)S(1)} %get-tuple-element.27), channel_id=1, source_target_pairs={{16,0},{17,1},{18,2},{19,3},{20,4},{21,5},{22,6},{23,7},{24,8},{25... | collective-permute-start | bytes 2359304 | tf_op jit(solution)/shard_map/ppermute | solution.py:83
  40.6 8.2 %copy-start.1 = (s32[128]{0:T(128)S(1)}, s32[128]{0:T(128)}, u32[]{:S(2)}) copy-start(s32[128]{0:T(128)} %param.5) | copy-start | bytes 1540
  40.6 41.6 %copy-start = (bf16[128,40]{0,1:T(8,128)(2,1)S(1)}, bf16[128,40]{0,1:T(8,128)(2,1)}, u32[]{:S(2)}) copy-start(bf16[128,40]{0,1:T(8,128)(2,1)} %param.6) | copy-start | bytes 30724
  42.9 63.5 %all-to-all-start = ((bf16[128,16,256]{0,2,1:T(8,128)(2,1)}), bf16[128,16,256]{0,2,1:T(8,128)(2,1)S(1)}, u32[]{:S(2)}, u32[]{:S(2)}) async-start(bf16[128,16,256]{0,2,1:T(8,128)(2,1)} %bitcast.4), calls=%async_computation | async-start | bytes 2097152 | tf_op jit(solution)/shard_map/all_to_all | solution.py:102

commit v2 on v1

v2 whole, which is shorter than its diff:
```python
import functools

import jax
import jax.numpy as jnp
from jax import lax
from jax.experimental import pallas as pl
from jax.experimental.pallas import tpu as pltpu
from jax.sharding import PartitionSpec as P

NSITE = 60
SITE_ROWS = 64
PASSES = 3
EB_ITERS = 5
CHUNKS = 4
SUB = 16
MESH = pl.DeviceIdType.MESH

center_weight = 0.1
along_weight = 0.35
across_weight = 0.05


def stencil(below, core, above, mask, inner_low, inner_high):
    along = above + below
    edge = jnp.zeros_like(core[:1])
    up = jnp.concatenate([core[1:], edge], axis=0)
    down = jnp.concatenate([edge, core[:-1]], axis=0)
    right = jnp.where(inner_high, pltpu.roll(core, core.shape[2] - 1, 2), 0.0)
    left = jnp.where(inner_low, pltpu.roll(core, 1, 2), 0.0)
    across = up + down + right + left
    mixed = center_weight * core + along_weight * along + across_weight * across
    return (mixed * mask).astype(jnp.bfloat16)


def body(
    covars, x, mask, mask_rows, pack, out,
    low, high, mask_low, mask_high, mask_wide, p1, p2, smooth, recv, gathered, flags, flags_t,
    tables, terms, group_terms, vox_terms,
    halo_send, halo_recv, mask_send, mask_recv, pack_send, pack_recv, data_send, data_recv,
    own_sem, term_send, term_recv, vox_send, vox_recv,
):
    layers, height, rows, width = x.shape
    chunk = rows // CHUNKS
    vox, vox_count = lax.axis_index("vox"), lax.axis_size("vox")
    nsite = lax.axis_size("site")
    members = lax.axis_size("subj") * nsite
    me = lax.axis_index("subj") * nsite + lax.axis_index("site")
    piece = layers * height // members

    def peer(step):
        return lax.rem(me + step, members)

    def group_id(index):
        return {"subj": index // nsite, "site": lax.rem(index, nsite)}

    def vox_peer(step):
        return lax.rem(vox + step, vox_count)

    barrier = pltpu.get_barrier_semaphore()

    @pl.loop(1, members)
    def _(step):
        pl.semaphore_signal(barrier, inc=1, device_id=group_id(peer(step)), device_id_type=MESH)

    @pl.loop(1, vox_count)
    def _(step):
        pl.semaphore_signal(barrier, inc=1, device_id={"vox": vox_peer(step)}, device_id_type=MESH)

    pl.semaphore_wait(barrier, members - 1 + vox_count - 1)

    def halo_up(c):
        rows_of = pl.ds(c * chunk, chunk)
        return pltpu.make_async_remote_copy(
            x.at[pl.ds(layers - PASSES, PASSES), :, rows_of], low.at[:, :, rows_of],
            halo_send.at[0, c], halo_recv.at[0, c], device_id={"vox": vox + 1}, device_id_type=MESH,
        )

    def halo_down(c):
        rows_of = pl.ds(c * chunk, chunk)
        return pltpu.make_async_remote_copy(
            x.at[pl.ds(0, PASSES), :, rows_of], high.at[:, :, rows_of],
            halo_send.at[1, c], halo_recv.at[1, c], device_id={"vox": vox - 1}, device_id_type=MESH,
        )

    mask_up = pltpu.make_async_remote_copy(
        mask.at[pl.ds(layers - PASSES, PASSES)], mask_low,
        mask_send.at[0], mask_recv.at[0], device_id={"vox": vox + 1}, device_id_type=MESH,
    )
    mask_down = pltpu.make_async_remote_copy(
        mask.at[pl.ds(0, PASSES)], mask_high,
        mask_send.at[1], mask_recv.at[1], device_id={"vox": vox - 1}, device_id_type=MESH,
    )
    has_up, has_down = vox < vox_count - 1, vox > 0

    @pl.when(has_up)
    def _():
        mask_up.start()
        for c in range(CHUNKS):
            halo_up(c).start()

    @pl.when(has_down)
    def _():
        mask_down.start()
        for c in range(CHUNKS):
            halo_down(c).start()

    def pack_copy(index):
        return pltpu.make_async_remote_copy(
            pack, gathered.at[me], pack_send, pack_recv,
            device_id=group_id(index), device_id_type=MESH,
        )

    @pl.loop(1, members)
    def _(step):
        pack_copy(peer(step)).start()

    gathered[me] = pack[...]

    @pl.when(jnp.logical_not(has_down))
    def _():
        low[...] = jnp.zeros_like(low)
        mask_low[...] = jnp.zeros_like(mask_low)

    @pl.when(jnp.logical_not(has_up))
    def _():
        high[...] = jnp.zeros_like(high)
        mask_high[...] = jnp.zeros_like(mask_high)

    @pl.when(has_down)
    def _():
        mask_up.wait_recv()

    @pl.when(has_up)
    def _():
        mask_down.wait_recv()

    def layer_of(low_ref, ref, high_ref, index):
        if index < PASSES:
            return low_ref.at[index]
        if index < PASSES + layers:
            return ref.at[index - PASSES]
        return high_ref.at[index - PASSES - layers]

    for index in range(layers + 2 * PASSES):
        values = layer_of(mask_low, mask, mask_high, index)[...]
        for y in range(height):
            mask_wide[index, y] = jnp.broadcast_to(values[y:y + 1], (SUB, width))

    lane = lax.broadcasted_iota(jnp.int32, (height, SUB, width), 2)
    inner_low, inner_high = lane > 0, lane < width - 1

    def send_piece(index, c):
        rows_of = pl.ds(c * chunk, chunk)
        return pltpu.make_async_remote_copy(
            smooth.at[pl.ds(index * piece, piece), rows_of], recv.at[me, :, rows_of],
            data_send, data_recv, device_id=group_id(index), device_id_type=MESH,
        )

    @pl.loop(0, CHUNKS)
    def _(c):
        @pl.when(has_down)
        def _():
            halo_up(c).wait_recv()

        @pl.when(has_up)
        def _():
            halo_down(c).wait_recv()

        @pl.loop(0, chunk // SUB)
        def _(b):
            rows_of = pl.ds(pl.multiple_of(c * chunk + b * SUB, SUB), SUB)
            sources = [layer_of(low, x, high, i) for i in range(layers + 2 * PASSES)]
            stage = [functools.partial(lambda ref: ref[:, rows_of], s) for s in sources]
            for step, target in enumerate((p1, p2, None)):
                count = layers + 2 * (PASSES - 1 - step)
                below = stage[0]().astype(jnp.float32)
                core = stage[1]().astype(jnp.float32)
                for i in range(count):
                    above = stage[i + 2]().astype(jnp.float32)
                    result = stencil(
                        below, core, above, mask_wide[i + 1 + step], inner_low, inner_high
                    )
                    if target is None:
                        smooth[pl.ds(i * height, height), rows_of] = result
                    else:
                        target[i] = result
                    below, core = core, above
                if target is not None:
                    stage = [functools.partial(lambda ref, k: ref[k], target, i) for i in range(count)]

        @pl.loop(1, members)
        def _(step):
            send_piece(peer(step), c).start()

    own = pltpu.make_async_copy(smooth.at[pl.ds(me * piece, piece)], recv.at[me], own_sem)
    own.start()

    others = pl.ds(0, members - 1)
    pltpu.make_async_copy(gathered.at[others], gathered.at[others], pack_recv).wait()
    site_row = lax.broadcasted_iota(jnp.int32, (width, rows), 0).astype(jnp.float32)
    counts = jnp.zeros((SITE_ROWS, 1), jnp.float32)
    for m in range(members):
        labels = gathered[m].astype(jnp.float32)[covars:covars + 1]
        flag = jnp.where(site_row == labels, 1.0, 0.0)
        counts = counts + jnp.sum(flag[:SITE_ROWS], axis=1, keepdims=True)
        flags_t[:, m * rows:(m + 1) * rows] = flag[:SITE_ROWS].astype(jnp.bfloat16)
        flags[m] = flag.T[:, :SITE_ROWS].astype(jnp.bfloat16)

    own.wait()
    pltpu.make_async_copy(recv.at[others], recv.at[others], data_recv).wait()

    firsts, seconds, weights = [], [], []
    for r in range(piece):
        data = recv[:, r].reshape(members * rows, width)
        values = data.astype(jnp.float32)
        square = (values * values).astype(jnp.bfloat16)
        firsts.append(jnp.dot(flags_t[...], data, preferred_element_type=jnp.float32))
        seconds.append(jnp.dot(flags_t[...], square, preferred_element_type=jnp.float32))
        weights.append(mask_rows[pl.ds(me * piece + r, 1), :])
    first = jnp.concatenate(firsts, axis=1)
    second = jnp.concatenate(seconds, axis=1)
    weight = jnp.concatenate(weights, axis=1)

    total = jnp.sum(counts)
    real = lax.broadcasted_iota(jnp.int32, (SITE_ROWS, 1), 0) < NSITE
    column = jnp.where(real, counts, 2.0)
    voxel_mean = jnp.sum(first, axis=0, keepdims=True) / total
    voxel_var = jnp.sum(second, axis=0, keepdims=True) / total - voxel_mean * voxel_mean + 1e-05
    deviation = jnp.sqrt(voxel_var)
    sum_z = (first - column * voxel_mean) / deviation
    sum_zz = (second - 2.0 * voxel_mean * first + column * voxel_mean * voxel_mean) / voxel_var
    gamma_hat = sum_z / column
    delta_hat = (sum_zz - sum_z * sum_z / column) / (column - 1.0)

    columns = (
        jnp.sum(weight * gamma_hat, axis=1, keepdims=True),
        jnp.sum(weight * gamma_hat * gamma_hat, axis=1, keepdims=True),
        jnp.sum(weight * delta_hat, axis=1, keepdims=True),
        jnp.sum(weight * delta_hat * delta_hat, axis=1, keepdims=True),
        jnp.broadcast_to(jnp.sum(weight, axis=1, keepdims=True), (SITE_ROWS, 1)),
    )
    place = lax.broadcasted_iota(jnp.int32, (SITE_ROWS, 128), 1)
    block = jnp.zeros((SITE_ROWS, 128), jnp.float32)
    for k, value in enumerate(columns):
        block = jnp.where(place == k, value, block)
    block = jnp.concatenate([block, jnp.zeros((128 - SITE_ROWS, 128), jnp.float32)], axis=0)
    terms[0] = block.T[:8]

    def term_copy(index):
        return pltpu.make_async_remote_copy(
            terms.at[0], group_terms.at[me], term_send, term_recv,
            device_id=group_id(index), device_id_type=MESH,
        )

    @pl.loop(1, members)
    def _(step):
        term_copy(peer(step)).start()

    group_terms[me] = terms[0]
    pltpu.make_async_copy(group_terms.at[others], group_terms.at[others], term_recv).wait()
    terms[1] = jnp.sum(group_terms[...], axis=0)

    def vox_copy(index):
        return pltpu.make_async_remote_copy(
            terms.at[1], vox_terms.at[vox], vox_send, vox_recv,
            device_id={"vox": index}, device_id_type=MESH,
        )

    @pl.loop(1, vox_count)
    def _(step):
        vox_copy(vox_peer(step)).start()

    vox_terms[vox] = terms[1]
    vox_others = pl.ds(0, vox_count - 1)
    pltpu.make_async_copy(vox_terms.at[vox_others], vox_terms.at[vox_others], vox_recv).wait()
    summed = jnp.sum(vox_terms[...], axis=0)
    summed = jnp.concatenate([summed, jnp.zeros((120, 128), jnp.float32)], axis=0).T[:SITE_ROWS]
    weight_total = summed[:, 4:5]

    gamma_bar = summed[:, 0:1] / weight_total
    tau_sq = summed[:, 1:2] / weight_total - gamma_bar * gamma_bar + 1e-06
    delta_mean = summed[:, 2:3] / weight_total
    delta_var = summed[:, 3:4] / weight_total - delta_mean * delta_mean + 1e-06
    shape_a = (2.0 * delta_var + delta_mean * delta_mean) / delta_var
    shape_b = (delta_mean * delta_var + delta_mean * delta_mean * delta_mean) / delta_var
    gamma_star, delta_star = gamma_hat, delta_hat
    for step in range(EB_ITERS):
        gamma_star = (column * tau_sq * gamma_hat + delta_star * gamma_bar) / (
            column * tau_sq + delta_star
        )
        spread = sum_zz - 2.0 * gamma_star * sum_z + column * gamma_star * gamma_star
        delta_star = (shape_b + 0.5 * spread) / (0.5 * column + shape_a - 1.0)
    cells = piece * width
    tables[:, :cells] = jnp.where(real, deviation * gamma_star, 0.0).astype(jnp.bfloat16)
    tables[:, cells:] = jnp.where(real, 1.0 / jnp.sqrt(delta_star), 0.0).astype(jnp.bfloat16)

    out[...] = jnp.zeros_like(out)

    @pl.loop(0, members)
    def _(m):
        picked = jnp.dot(flags[m], tables[...], preferred_element_type=jnp.float32)
        values = jnp.concatenate([recv[m, r] for r in range(piece)], axis=1).astype(jnp.float32)
        adjusted = (values - voxel_mean - picked[:, :cells]) * picked[:, cells:] + voxel_mean
        product = jnp.dot(
            gathered[m], adjusted.astype(jnp.bfloat16), preferred_element_type=jnp.float32
        )
        out[...] += product[:covars]

    @pl.when(has_up)
    def _():
        mask_up.wait_send()
        for c in range(CHUNKS):
            halo_up(c).wait_send()

    @pl.when(has_down)
    def _():
        mask_down.wait_send()
        for c in range(CHUNKS):
            halo_down(c).wait_send()

    pltpu.make_async_copy(gathered.at[others], gathered.at[others], pack_send).wait()
    pltpu.make_async_copy(recv.at[others], recv.at[others], data_send).wait()
    pltpu.make_async_copy(group_terms.at[others], group_terms.at[others], term_send).wait()
    pltpu.make_async_copy(vox_terms.at[vox_others], vox_terms.at[vox_others], vox_send).wait()


def per_device(voxel_data, site_label, covariates, brain_mask):
    rows, layers, height, width = voxel_data.shape
    covars = covariates.shape[1]
    members = lax.axis_size("subj") * lax.axis_size("site")
    vox_count = lax.axis_size("vox")
    piece = layers * height // members
    pack_rows = -(-(covars + 1) // 16) * 16
    x = jnp.transpose(voxel_data, (1, 2, 0, 3))
    mask = brain_mask.astype(jnp.float32)
    pack = jnp.concatenate(
        [
            covariates.T,
            site_label[None].astype(jnp.bfloat16),
            jnp.zeros((pack_rows - covars - 1, rows), jnp.bfloat16),
        ]
    )
    bf16, f32 = jnp.bfloat16, jnp.float32
    return pl.pallas_call(
        functools.partial(body, covars),
        out_shape=jax.ShapeDtypeStruct((covars, piece * width), f32),
        in_specs=[pl.BlockSpec(memory_space=pltpu.VMEM)] * 4,
        out_specs=pl.BlockSpec(memory_space=pltpu.VMEM),
        scratch_shapes=[
            pltpu.VMEM((PASSES, height, rows, width), bf16),
            pltpu.VMEM((PASSES, height, rows, width), bf16),
            pltpu.VMEM((PASSES, height, width), f32),
            pltpu.VMEM((PASSES, height, width), f32),
            pltpu.VMEM((layers + 2 * PASSES, height, SUB, width), f32),
            pltpu.VMEM((layers + 4, height, SUB, width), bf16),
            pltpu.VMEM((layers + 2, height, SUB, width), bf16),
            pltpu.VMEM((layers * height, rows, width), bf16),
            pltpu.VMEM((members, piece, rows, width), bf16),
            pltpu.VMEM((members, pack_rows, rows), bf16),
            pltpu.VMEM((members, rows, SITE_ROWS), bf16),
            pltpu.VMEM((SITE_ROWS, members * rows), bf16),
            pltpu.VMEM((SITE_ROWS, 2 * piece * width), bf16),
            pltpu.VMEM((2, 8, 128), f32),
            pltpu.VMEM((members, 8, 128), f32),
            pltpu.VMEM((vox_count, 8, 128), f32),
            pltpu.SemaphoreType.DMA((2, CHUNKS)),
            pltpu.SemaphoreType.DMA((2, CHUNKS)),
            pltpu.SemaphoreType.DMA((2,)),
            pltpu.SemaphoreType.DMA((2,)),
        ]
        + [pltpu.SemaphoreType.DMA(())] * 9,
        compiler_params=pltpu.CompilerParams(
            collective_id=0, has_side_effects=True, vmem_limit_bytes=40 * 1024 * 1024
        ),
    )(x, mask, mask.reshape(layers * height, width), pack)


def solution(mesh):
    in_specs = (
        P(("subj", "site"), "vox", None, None),
        P(("subj", "site")),
        P(("subj", "site"), None),
        P("vox", None, None),
    )
    out_specs = P(None, ("vox", "subj", "site"))
    return jax.shard_map(
        per_device, mesh=mesh, in_specs=in_specs, out_specs=out_specs, check_vma=False
    )
```

time: 152 us -> 55 us (0.36)
  blocking collectives: 92.2 us -> 0 us
  Pallas kernels: 0 us -> 51 us
  waiting for transfers between devices: 19 us -> 0 us
  starting transfers between devices: 17.9 us -> 0 us
  other arithmetic: 13 us -> 1.45 us
  matrix products: 3.01 us -> 0 us
  local copies, waits for them, and re-layouts: 4.94 us -> 2.34 us
    all_gather x2 -> x0, blocking collectives: 55.3 us -> none  [the longest x1 33.3 us: per_device(): labels = lax.all_gather(site_label, group, tiled=True)]
    pallas_call x0 -> x1, Pallas kernels: none -> 51 us  [per_device(): pl.pallas_call(functools.partial(body, covars), out_shape=jax.ShapeDtypeS...]
    psum x1 -> x0, blocking collectives: 36.9 us -> none  [per_device(): packed = lax.psum(packed, ('vox', 'subj', 'site'))]
    ppermute x4 -> x0, waiting for transfers between devices: 19 us -> none  [the longest x2 14.8 us: widen(): lax.ppermute(lax.slice_in_dim(block, block.shape[1] - width, None, axis=1...]
    ppermute x4 -> x0, starting transfers between devices: 12 us -> none  [the longest x2 9.45 us: widen(): lax.ppermute(lax.slice_in_dim(block, block.shape[1] - width, None, axis=1...]
    convert_element_type x5 -> x1, other arithmetic: 7.82 us -> 0.67 us  [per_device(): site_label[None].astype(jnp.bfloat16)]
    all_to_all x1 -> x0, starting transfers between devices: 5.91 us -> none  [per_device(): lax.all_to_all(smoothed, group, 1, 0, tiled=True)]
    dot_general x4 -> x0, matrix products: 3.01 us -> none  [the longest x1 1.67 us: per_device(): return jnp.dot(covs.T, adjusted, preferred_element_type=jnp.float32)]
  transfers between devices with their start and end apart: 5 -> 0, of which waited for: 2 -> 0; matrix products, arithmetic and copies ran while one was open for 3% -> 0% of each run, Pallas kernels for 0% -> 0%
where the time goes in v2:
time: 55 us; the launch traced here: 54.8 us
  Pallas kernels  51 us (93%)
  local copies, waits for them, and re-layouts  2.34 us (4%)
  other arithmetic  1.45 us (3%)
    pallas_call x1, Pallas kernels, per_device(): pl.pallas_call(functools.partial(body, covars), out_shape=jax.ShapeDtypeS...  51 us
    unnamed x4, local copies, waits for them, and re-layouts  2.26 us

profile of v2, /device:TPU:0, one launch (start us, length us, event | category | flops | bytes accessed | tf_op | source)
XLA Modules:
  0.0 54.8 jit_solution(15723610058636036246)
XLA Ops:
  0.0 0.0 copy-start
  0.0 0.7 %convert_bitcast_fusion = bf16[1,128]{1,0:T(2,128)(2,1)S(1)} fusion(s32[128]{0:T(128)} %param.5), kind=kLoop, calls=%fused_computation.2 | loop fusion | flops 128 | bytes 768 | tf_op jit(solution)/shard_map/convert_element_type | solution.py:339
  0.7 0.1 pad.2.clone
  0.8 0.8 %maximum_maximum_fusion.pack = bf16[48,128]{1,0:T(8,128)(2,1)S(1)} fusion(bf16[1,128]{1,0:T(2,128)(2,1)S(1)} %convert_bitcast_fusion, bf16[40,128]{1,0:T(8,128)(2,1)} %bitcast.9, bf16[48]{0:T(256)(128)(2,1)S(1)} %pad.2.clone), kind=kLoop, calls=%fused_computation.1 | loop fusion | flops 36864 | bytes 22880 | tf_op jit(solution)/shard_map/concatenate | solution.py:336
  1.5 0.0 copy-done
  1.5 1.6 %copy.7 = bf16[128,4,8,128]{3,0,2,1:T(8,128)(2,1)S(1)} copy(bf16[128,4,8,128]{3,2,1,0:T(8,128)(2,1)} %param.4) | data formatting | bytes 2097152 | tf_op args[0]
  3.2 51.0 %shard_map.46 = f32[40,256]{1,0:T(8,128)S(1)} custom-call(bf16[4,8,128,128]{3,2,1,0:T(8,128)(2,1)S(1)} %bitcast.8, f32[4,8,128]{2,1,0:T(8,128)S(1)} %get-tuple-element.6.mask, f32[32,128]{1,0:T(8,128)S(1)} %get-tuple-element.5.mask_rows, bf16[48,128]{1,0:T(8,128)(2,1)S(1)} %maximum_maximum_fusion.pack), custom_call_target="tpu_custom_call" | custom-call | tf_op jit(solution)/shard_map/pallas_call | solution.py:344
  54.2 0.6 %copy.9 = f32[40,256]{1,0:T(8,128)} copy(f32[40,256]{1,0:T(8,128)S(1)} %shard_map.46) | data formatting | bytes 81920
  (2 shorter events, 0.0 us)
Async XLA Ops:
  0.0 1.5 %copy-start = (s32[4,8,128]{2,1,0:T(8,128)S(1)}, s32[4,8,128]{2,1,0:T(8,128)}, u32[]{:S(2)}) copy-start(s32[4,8,128]{2,1,0:T(8,128)} %param.7) | copy-start | bytes 49156

commit v3 on v2

--- a/solution.py
+++ b/solution.py
@@ -11,7 +11,7 @@
 SITE_ROWS = 64
 PASSES = 3
 EB_ITERS = 5
-CHUNKS = 4
+CHUNKS = 8
 SUB = 16
 MESH = pl.DeviceIdType.MESH
 
@@ -34,10 +34,10 @@
 
 def body(
     covars, x, mask, mask_rows, pack, out,
-    low, high, mask_low, mask_high, mask_wide, p1, p2, smooth, recv, gathered, flags, flags_t,
-    tables, terms, group_terms, vox_terms,
+    low, high, mask_low, mask_high, mask_wide, p1, p2, smooth, recv, gathered, covs, flags_wide,
+    flags, flags_t, moments, tables, terms, all_terms,
     halo_send, halo_recv, mask_send, mask_recv, pack_send, pack_recv, data_send, data_recv,
-    own_sem, term_send, term_recv, vox_send, vox_recv,
+    own_sem, term_send, term_recv,
 ):
     layers, height, rows, width = x.shape
     chunk = rows // CHUNKS
@@ -53,20 +53,21 @@
     def group_id(index):
         return {"subj": index // nsite, "site": lax.rem(index, nsite)}
 
-    def vox_peer(step):
-        return lax.rem(vox + step, vox_count)
-
     barrier = pltpu.get_barrier_semaphore()
 
-    @pl.loop(1, members)
+    everyone = vox_count * members
+    my_id = vox * members + me
+
+    def any_id(step):
+        index = lax.rem(my_id + step, everyone)
+        member = lax.rem(index, members)
+        return {"vox": index // members, "subj": member // nsite, "site": lax.rem(member, nsite)}
+
+    @pl.loop(1, everyone)
     def _(step):
-        pl.semaphore_signal(barrier, inc=1, device_id=group_id(peer(step)), device_id_type=MESH)
-
-    @pl.loop(1, vox_count)
-    def _(step):
-        pl.semaphore_signal(barrier, inc=1, device_id={"vox": vox_peer(step)}, device_id_type=MESH)
-
-    pl.semaphore_wait(barrier, members - 1 + vox_count - 1)
+        pl.semaphore_signal(barrier, inc=1, device_id=any_id(step), device_id_type=MESH)
+
+    pl.semaphore_wait(barrier, everyone - 1)
 
     def halo_up(c):
         rows_of = pl.ds(c * chunk, chunk)
@@ -153,7 +154,7 @@
         rows_of = pl.ds(c * chunk, chunk)
         return pltpu.make_async_remote_copy(
             smooth.at[pl.ds(index * piece, piece), rows_of], recv.at[me, :, rows_of],
-            data_send, data_recv, device_id=group_id(index), device_id_type=MESH,
+            data_send, data_recv.at[c], device_id=group_id(index), device_id_type=MESH,
         )
 
     @pl.loop(0, CHUNKS)
@@ -200,26 +201,39 @@
     site_row = lax.broadcasted_iota(jnp.int32, (width, rows), 0).astype(jnp.float32)
     counts = jnp.zeros((SITE_ROWS, 1), jnp.float32)
     for m in range(members):
-        labels = gathered[m].astype(jnp.float32)[covars:covars + 1]
+        block = gathered[m]
+        labels = block.astype(jnp.float32)[covars:covars + 1]
         flag = jnp.where(site_row == labels, 1.0, 0.0)
         counts = counts + jnp.sum(flag[:SITE_ROWS], axis=1, keepdims=True)
-        flags_t[:, m * rows:(m + 1) * rows] = flag[:SITE_ROWS].astype(jnp.bfloat16)
-        flags[m] = flag.T[:, :SITE_ROWS].astype(jnp.bfloat16)
-
+        turned = flag.T
+        flags_wide[m] = turned
+        flags[m * rows:(m + 1) * rows] = turned[:, :SITE_ROWS].astype(jnp.bfloat16)
+        covs[:, m * rows:(m + 1) * rows] = block
+    for c in range(CHUNKS):
+        part = flags_wide[:, c * chunk:(c + 1) * chunk].reshape(members * chunk, width)
+        flags_t[c] = part.T[:SITE_ROWS].astype(jnp.bfloat16)
+
+    cells = piece * width
+    moments[...] = jnp.zeros_like(moments)
     own.wait()
-    pltpu.make_async_copy(recv.at[others], recv.at[others], data_recv).wait()
-
-    firsts, seconds, weights = [], [], []
-    for r in range(piece):
-        data = recv[:, r].reshape(members * rows, width)
+
+    @pl.loop(0, CHUNKS)
+    def _(c):
+        arrived = recv.at[others, :, pl.ds(0, chunk)]
+        pltpu.make_async_copy(arrived, arrived, data_recv.at[c]).wait()
+        rows_of = pl.ds(pl.multiple_of(c * chunk, chunk), chunk)
+        data = jnp.concatenate(
+            [recv[:, r, rows_of].reshape(members * chunk, width) for r in range(piece)], axis=1
+        )
         values = data.astype(jnp.float32)
         square = (values * values).astype(jnp.bfloat16)
-        firsts.append(jnp.dot(flags_t[...], data, preferred_element_type=jnp.float32))
-        seconds.append(jnp.dot(flags_t[...], square, preferred_element_type=jnp.float32))
-        weights.append(mask_rows[pl.ds(me * piece + r, 1), :])
-    first = jnp.concatenate(firsts, axis=1)
-    second = jnp.concatenate(seconds, axis=1)
-    weight = jnp.concatenate(weights, axis=1)
+        moments[:, :cells] += jnp.dot(flags_t[c], data, preferred_element_type=jnp.float32)
+        moments[:, cells:] += jnp.dot(flags_t[c], square, preferred_element_type=jnp.float32)
+
+    first, second = moments[:, :cells], moments[:, cells:]
+    weight = jnp.concatenate(
+        [mask_rows[pl.ds(me * piece + r, 1), :] for r in range(piece)], axis=1
+    )
 
     total = jnp.sum(counts)
     real = lax.broadcasted_iota(jnp.int32, (SITE_ROWS, 1), 0) < NSITE
@@ -244,36 +258,22 @@
     for k, value in enumerate(columns):
         block = jnp.where(place == k, value, block)
     block = jnp.concatenate([block, jnp.zeros((128 - SITE_ROWS, 128), jnp.float32)], axis=0)
-    terms[0] = block.T[:8]
-
-    def term_copy(index):
-        return pltpu.make_async_remote_copy(
-            terms.at[0], group_terms.at[me], term_send, term_recv,
-            device_id=group_id(index), device_id_type=MESH,
-        )
-
-    @pl.loop(1, members)
+    terms[...] = block.T[:8]
+
+    def term_copy(step):
+        return pltpu.make_async_remote_copy(
+            terms, all_terms.at[my_id], term_send, term_recv,
+            device_id=any_id(step), device_id_type=MESH,
+        )
+
+    @pl.loop(1, everyone)
     def _(step):
-        term_copy(peer(step)).start()
-
-    group_terms[me] = terms[0]
-    pltpu.make_async_copy(group_terms.at[others], group_terms.at[others], term_recv).wait()
-    terms[1] = jnp.sum(group_terms[...], axis=0)
-
-    def vox_copy(index):
-        return pltpu.make_async_remote_copy(
-            terms.at[1], vox_terms.at[vox], vox_send, vox_recv,
-            device_id={"vox": index}, device_id_type=MESH,
-        )
-
-    @pl.loop(1, vox_count)
-    def _(step):
-        vox_copy(vox_peer(step)).start()
-
-    vox_terms[vox] = terms[1]
-    vox_others = pl.ds(0, vox_count - 1)
-    pltpu.make_async_copy(vox_terms.at[vox_others], vox_terms.at[vox_others], vox_recv).wait()
-    summed = jnp.sum(vox_terms[...], axis=0)
+        term_copy(step).start()
+
+    all_terms[my_id] = terms[...]
+    all_others = pl.ds(0, everyone - 1)
+    pltpu.make_async_copy(all_terms.at[all_others], all_terms.at[all_others], term_recv).wait()
+    summed = jnp.sum(all_terms[...], axis=0)
     summed = jnp.concatenate([summed, jnp.zeros((120, 128), jnp.float32)], axis=0).T[:SITE_ROWS]
     weight_total = summed[:, 4:5]
 
@@ -284,27 +284,31 @@
     shape_a = (2.0 * delta_var + delta_mean * delta_mean) / delta_var
     shape_b = (delta_mean * delta_var + delta_mean * delta_mean * delta_mean) / delta_var
     gamma_star, delta_star = gamma_hat, delta_hat
+    prior = column * tau_sq
+    pulled = prior * gamma_hat
+    inverse = 1.0 / (0.5 * column + shape_a - 1.0)
     for step in range(EB_ITERS):
-        gamma_star = (column * tau_sq * gamma_hat + delta_star * gamma_bar) / (
-            column * tau_sq + delta_star
-        )
+        gamma_star = (pulled + delta_star * gamma_bar) / (prior + delta_star)
         spread = sum_zz - 2.0 * gamma_star * sum_z + column * gamma_star * gamma_star
-        delta_star = (shape_b + 0.5 * spread) / (0.5 * column + shape_a - 1.0)
-    cells = piece * width
+        delta_star = (shape_b + 0.5 * spread) * inverse
     tables[:, :cells] = jnp.where(real, deviation * gamma_star, 0.0).astype(jnp.bfloat16)
     tables[:, cells:] = jnp.where(real, 1.0 / jnp.sqrt(delta_star), 0.0).astype(jnp.bfloat16)
 
-    out[...] = jnp.zeros_like(out)
-
-    @pl.loop(0, members)
-    def _(m):
-        picked = jnp.dot(flags[m], tables[...], preferred_element_type=jnp.float32)
-        values = jnp.concatenate([recv[m, r] for r in range(piece)], axis=1).astype(jnp.float32)
+    pair = 2 if members % 2 == 0 else 1
+    product = None
+    for g in range(members // pair):
+        span = slice(g * pair * rows, (g + 1) * pair * rows)
+        picked = jnp.dot(flags[span], tables[...], preferred_element_type=jnp.float32)
+        values = jnp.concatenate(
+            [recv[g * pair:(g + 1) * pair, r].reshape(pair * rows, width) for r in range(piece)],
+            axis=1,
+        ).astype(jnp.float32)
         adjusted = (values - voxel_mean - picked[:, :cells]) * picked[:, cells:] + voxel_mean
-        product = jnp.dot(
-            gathered[m], adjusted.astype(jnp.bfloat16), preferred_element_type=jnp.float32
-        )
-        out[...] += product[:covars]
+        partial = jnp.dot(
+            covs[:, span], adjusted.astype(jnp.bfloat16), preferred_element_type=jnp.float32
+        )
+        product = partial if product is None else product + partial
+    out[...] = product[:covars]
 
     @pl.when(has_up)
     def _():
@@ -320,8 +324,7 @@
 
     pltpu.make_async_copy(gathered.at[others], gathered.at[others], pack_send).wait()
     pltpu.make_async_copy(recv.at[others], recv.at[others], data_send).wait()
-    pltpu.make_async_copy(group_terms.at[others], group_terms.at[others], term_send).wait()
-    pltpu.make_async_copy(vox_terms.at[vox_others], vox_terms.at[vox_others], vox_send).wait()
+    pltpu.make_async_copy(all_terms.at[all_others], all_terms.at[all_others], term_send).wait()
 
 
 def per_device(voxel_data, site_label, covariates, brain_mask):
@@ -357,18 +360,22 @@
             pltpu.VMEM((layers * height, rows, width), bf16),
             pltpu.VMEM((members, piece, rows, width), bf16),
             pltpu.VMEM((members, pack_rows, rows), bf16),
-            pltpu.VMEM((members, rows, SITE_ROWS), bf16),
-            pltpu.VMEM((SITE_ROWS, members * rows), bf16),
+            pltpu.VMEM((pack_rows, members * rows), bf16),
+            pltpu.VMEM((members, rows, width), f32),
+            pltpu.VMEM((members * rows, SITE_ROWS), bf16),
+            pltpu.VMEM((CHUNKS, SITE_ROWS, members * rows // CHUNKS), bf16),
+            pltpu.VMEM((SITE_ROWS, 2 * piece * width), f32),
             pltpu.VMEM((SITE_ROWS, 2 * piece * width), bf16),
-            pltpu.VMEM((2, 8, 128), f32),
-            pltpu.VMEM((members, 8, 128), f32),
-            pltpu.VMEM((vox_count, 8, 128), f32),
+            pltpu.VMEM((8, 128), f32),
+            pltpu.VMEM((vox_count * members, 8, 128), f32),
             pltpu.SemaphoreType.DMA((2, CHUNKS)),
             pltpu.SemaphoreType.DMA((2, CHUNKS)),
             pltpu.SemaphoreType.DMA((2,)),
             pltpu.SemaphoreType.DMA((2,)),
         ]
-        + [pltpu.SemaphoreType.DMA(())] * 9,
+        + [pltpu.SemaphoreType.DMA(())] * 3
+        + [pltpu.SemaphoreType.DMA((CHUNKS,))]
+        + [pltpu.SemaphoreType.DMA(())] * 3,
         compiler_params=pltpu.CompilerParams(
             collective_id=0, has_side_effects=True, vmem_limit_bytes=40 * 1024 * 1024
         ),

time: 55 us -> 48.9 us (0.89)
  Pallas kernels: 51 us -> 44.8 us
    pallas_call x1, Pallas kernels: 51 us -> 44.8 us  [per_device(): pl.pallas_call(functools.partial(body, covars), out_shape=jax.ShapeDtypeS...]
where the time goes in v3:
time: 48.9 us; the launch traced here: 48.6 us
  Pallas kernels  44.8 us (92%)
  local copies, waits for them, and re-layouts  2.34 us (5%)
  other arithmetic  1.45 us (3%)
    pallas_call x1, Pallas kernels, per_device(): pl.pallas_call(functools.partial(body, covars), out_shape=jax.ShapeDtypeS...  44.8 us
    unnamed x4, local copies, waits for them, and re-layouts  2.26 us

profile of v3, /device:TPU:0, one launch (start us, length us, event | category | flops | bytes accessed | tf_op | source)
XLA Modules:
  0.0 48.6 jit_solution(5773976218594878984)
XLA Ops:
  0.0 0.0 copy-start
  0.0 0.7 %convert_bitcast_fusion = bf16[1,128]{1,0:T(2,128)(2,1)S(1)} fusion(s32[128]{0:T(128)} %param.5), kind=kLoop, calls=%fused_computation.2 | loop fusion | flops 128 | bytes 768 | tf_op jit(solution)/shard_map/convert_element_type | solution.py:342
  0.7 0.1 pad.2.clone
  0.8 0.8 %maximum_maximum_fusion.pack = bf16[48,128]{1,0:T(8,128)(2,1)S(1)} fusion(bf16[1,128]{1,0:T(2,128)(2,1)S(1)} %convert_bitcast_fusion, bf16[40,128]{1,0:T(8,128)(2,1)} %bitcast.9, bf16[48]{0:T(256)(128)(2,1)S(1)} %pad.2.clone), kind=kLoop, calls=%fused_computation.1 | loop fusion | flops 36864 | bytes 22880 | tf_op jit(solution)/shard_map/concatenate | solution.py:339
  1.5 0.0 copy-done
  1.5 1.6 %copy.7 = bf16[128,4,8,128]{3,0,2,1:T(8,128)(2,1)S(1)} copy(bf16[128,4,8,128]{3,2,1,0:T(8,128)(2,1)} %param.4) | data formatting | bytes 2097152 | tf_op args[0]
  3.2 44.8 %shard_map.46 = f32[40,256]{1,0:T(8,128)S(1)} custom-call(bf16[4,8,128,128]{3,2,1,0:T(8,128)(2,1)S(1)} %bitcast.8, f32[4,8,128]{2,1,0:T(8,128)S(1)} %get-tuple-element.6.mask, f32[32,128]{1,0:T(8,128)S(1)} %get-tuple-element.5.mask_rows, bf16[48,128]{1,0:T(8,128)(2,1)S(1)} %maximum_maximum_fusion.pack), custom_call_target="tpu_custom_call" | custom-call | tf_op jit(solution)/shard_map/pallas_call | solution.py:347
  48.0 0.6 %copy.9 = f32[40,256]{1,0:T(8,128)} copy(f32[40,256]{1,0:T(8,128)S(1)} %shard_map.46) | data formatting | bytes 81920
  (2 shorter events, 0.0 us)
Async XLA Ops:
  0.0 1.5 %copy-start = (s32[4,8,128]{2,1,0:T(8,128)S(1)}, s32[4,8,128]{2,1,0:T(8,128)}, u32[]{:S(2)}) copy-start(s32[4,8,128]{2,1,0:T(8,128)} %param.7) | copy-start | bytes 49156

commit v4 on v3

--- a/solution.py
+++ b/solution.py
@@ -36,7 +36,8 @@
     covars, x, mask, mask_rows, pack, out,
     low, high, mask_low, mask_high, mask_wide, p1, p2, smooth, recv, gathered, covs, flags_wide,
     flags, flags_t, moments, tables, terms, all_terms,
-    halo_send, halo_recv, mask_send, mask_recv, pack_send, pack_recv, data_send, data_recv,
+    halo_send, halo_recv, mask_send, mask_recv, pack_send, pack_recv, fan_send, fan_recv,
+    data_send, data_recv,
     own_sem, term_send, term_recv,
 ):
     layers, height, rows, width = x.shape
@@ -105,17 +106,28 @@
         for c in range(CHUNKS):
             halo_down(c).start()
 
-    def pack_copy(index):
-        return pltpu.make_async_remote_copy(
-            pack, gathered.at[me], pack_send, pack_recv,
-            device_id=group_id(index), device_id_type=MESH,
-        )
-
-    @pl.loop(1, members)
+    nsubj = lax.axis_size("subj")
+    subj, site = lax.axis_index("subj"), lax.axis_index("site")
+    blocks = gathered.at[0, pl.ds(0, nsubj - 1)]
+    lines = gathered.at[pl.ds(0, nsite - 1)]
+
+    def pack_copy(step):
+        return pltpu.make_async_remote_copy(
+            pack, gathered.at[site, subj], pack_send, pack_recv,
+            device_id={"subj": lax.rem(subj + step, nsubj)}, device_id_type=MESH,
+        )
+
+    def fan_copy(step):
+        return pltpu.make_async_remote_copy(
+            gathered.at[site], gathered.at[site], fan_send, fan_recv,
+            device_id={"site": lax.rem(site + step, nsite)}, device_id_type=MESH,
+        )
+
+    @pl.loop(1, nsubj)
     def _(step):
-        pack_copy(peer(step)).start()
-
-    gathered[me] = pack[...]
+        pack_copy(step).start()
+
+    gathered[site, subj] = pack[...]
 
     @pl.when(jnp.logical_not(has_down))
     def _():
@@ -191,17 +203,25 @@
 
         @pl.loop(1, members)
         def _(step):
-            send_piece(peer(step), c).start()
+            send_piece(peer(members - step), c).start()
+
+        @pl.when(c == 0)
+        def _():
+            pltpu.make_async_copy(blocks, blocks, pack_recv).wait()
+
+            @pl.loop(1, nsite)
+            def _(step):
+                fan_copy(step).start()
 
     own = pltpu.make_async_copy(smooth.at[pl.ds(me * piece, piece)], recv.at[me], own_sem)
     own.start()
 
     others = pl.ds(0, members - 1)
-    pltpu.make_async_copy(gathered.at[others], gathered.at[others], pack_recv).wait()
+    pltpu.make_async_copy(lines, lines, fan_recv).wait()
     site_row = lax.broadcasted_iota(jnp.int32, (width, rows), 0).astype(jnp.float32)
     counts = jnp.zeros((SITE_ROWS, 1), jnp.float32)
     for m in range(members):
-        block = gathered[m]
+        block = gathered[m % nsite, m // nsite]
         labels = block.astype(jnp.float32)[covars:covars + 1]
         flag = jnp.where(site_row == labels, 1.0, 0.0)
         counts = counts + jnp.sum(flag[:SITE_ROWS], axis=1, keepdims=True)
@@ -246,19 +266,25 @@
     gamma_hat = sum_z / column
     delta_hat = (sum_zz - sum_z * sum_z / column) / (column - 1.0)
 
-    columns = (
-        jnp.sum(weight * gamma_hat, axis=1, keepdims=True),
-        jnp.sum(weight * gamma_hat * gamma_hat, axis=1, keepdims=True),
-        jnp.sum(weight * delta_hat, axis=1, keepdims=True),
-        jnp.sum(weight * delta_hat * delta_hat, axis=1, keepdims=True),
-        jnp.broadcast_to(jnp.sum(weight, axis=1, keepdims=True), (SITE_ROWS, 1)),
-    )
-    place = lax.broadcasted_iota(jnp.int32, (SITE_ROWS, 128), 1)
-    block = jnp.zeros((SITE_ROWS, 128), jnp.float32)
-    for k, value in enumerate(columns):
-        block = jnp.where(place == k, value, block)
-    block = jnp.concatenate([block, jnp.zeros((128 - SITE_ROWS, 128), jnp.float32)], axis=0)
-    terms[...] = block.T[:8]
+    gammas = weight * gamma_hat
+    deltas = weight * delta_hat
+    gamma_sums = jnp.concatenate(
+        [
+            jnp.sum(gammas, axis=1, keepdims=True),
+            jnp.sum(gammas * gamma_hat, axis=1, keepdims=True),
+        ]
+    )
+    delta_sums = jnp.concatenate(
+        [
+            jnp.sum(deltas, axis=1, keepdims=True),
+            jnp.sum(deltas * delta_hat, axis=1, keepdims=True),
+        ]
+    )
+    row = lax.broadcasted_iota(jnp.int32, (2 * SITE_ROWS, 1), 0)
+    gamma_sums = jnp.where(row == NSITE, jnp.sum(weight, axis=1, keepdims=True), gamma_sums)
+    place = lax.broadcasted_iota(jnp.int32, (128, 128), 1)
+    block = jnp.where(place == 0, gamma_sums, jnp.where(place == 1, delta_sums, 0.0))
+    terms[...] = block.T[:2]
 
     def term_copy(step):
         return pltpu.make_async_remote_copy(
@@ -274,13 +300,13 @@
     all_others = pl.ds(0, everyone - 1)
     pltpu.make_async_copy(all_terms.at[all_others], all_terms.at[all_others], term_recv).wait()
     summed = jnp.sum(all_terms[...], axis=0)
-    summed = jnp.concatenate([summed, jnp.zeros((120, 128), jnp.float32)], axis=0).T[:SITE_ROWS]
-    weight_total = summed[:, 4:5]
-
-    gamma_bar = summed[:, 0:1] / weight_total
-    tau_sq = summed[:, 1:2] / weight_total - gamma_bar * gamma_bar + 1e-06
-    delta_mean = summed[:, 2:3] / weight_total
-    delta_var = summed[:, 3:4] / weight_total - delta_mean * delta_mean + 1e-06
+    weight_total = summed[0:1, NSITE:NSITE + 1]
+    summed = jnp.concatenate([summed, jnp.zeros((126, 128), jnp.float32)], axis=0).T
+
+    gamma_bar = summed[:SITE_ROWS, 0:1] / weight_total
+    tau_sq = summed[SITE_ROWS:, 0:1] / weight_total - gamma_bar * gamma_bar + 1e-06
+    delta_mean = summed[:SITE_ROWS, 1:2] / weight_total
+    delta_var = summed[SITE_ROWS:, 1:2] / weight_total - delta_mean * delta_mean + 1e-06
     shape_a = (2.0 * delta_var + delta_mean * delta_mean) / delta_var
     shape_b = (delta_mean * delta_var + delta_mean * delta_mean * delta_mean) / delta_var
     gamma_star, delta_star = gamma_hat, delta_hat
@@ -322,7 +348,8 @@
         for c in range(CHUNKS):
             halo_down(c).wait_send()
 
-    pltpu.make_async_copy(gathered.at[others], gathered.at[others], pack_send).wait()
+    pltpu.make_async_copy(blocks, blocks, pack_send).wait()
+    pltpu.make_async_copy(lines, lines, fan_send).wait()
     pltpu.make_async_copy(recv.at[others], recv.at[others], data_send).wait()
     pltpu.make_async_copy(all_terms.at[all_others], all_terms.at[all_others], term_send).wait()
 
@@ -359,21 +386,21 @@
             pltpu.VMEM((layers + 2, height, SUB, width), bf16),
             pltpu.VMEM((layers * height, rows, width), bf16),
             pltpu.VMEM((members, piece, rows, width), bf16),
-            pltpu.VMEM((members, pack_rows, rows), bf16),
+            pltpu.VMEM((lax.axis_size("site"), lax.axis_size("subj"), pack_rows, rows), bf16),
             pltpu.VMEM((pack_rows, members * rows), bf16),
             pltpu.VMEM((members, rows, width), f32),
             pltpu.VMEM((members * rows, SITE_ROWS), bf16),
             pltpu.VMEM((CHUNKS, SITE_ROWS, members * rows // CHUNKS), bf16),
             pltpu.VMEM((SITE_ROWS, 2 * piece * width), f32),
             pltpu.VMEM((SITE_ROWS, 2 * piece * width), bf16),
-            pltpu.VMEM((8, 128), f32),
-            pltpu.VMEM((vox_count * members, 8, 128), f32),
+            pltpu.VMEM((2, 128), f32),
+            pltpu.VMEM((vox_count * members, 2, 128), f32),
             pltpu.SemaphoreType.DMA((2, CHUNKS)),
             pltpu.SemaphoreType.DMA((2, CHUNKS)),
             pltpu.SemaphoreType.DMA((2,)),
             pltpu.SemaphoreType.DMA((2,)),
         ]
-        + [pltpu.SemaphoreType.DMA(())] * 3
+        + [pltpu.SemaphoreType.DMA(())] * 5
         + [pltpu.SemaphoreType.DMA((CHUNKS,))]
         + [pltpu.SemaphoreType.DMA(())] * 3,
         compiler_params=pltpu.CompilerParams(

time: 48.9 us -> 47.3 us (0.967)
  Pallas kernels: 44.8 us -> 43.2 us
    pallas_call x1, Pallas kernels: 44.8 us -> 43.2 us  [per_device(): pl.pallas_call(functools.partial(body, covars), out_shape=jax.ShapeDtypeS...]
where the time goes in v4:
time: 47.3 us; the launch traced here: 47 us
  Pallas kernels  43.2 us (91%)
  local copies, waits for them, and re-layouts  2.34 us (5%)
  other arithmetic  1.45 us (3%)
    pallas_call x1, Pallas kernels, per_device(): pl.pallas_call(functools.partial(body, covars), out_shape=jax.ShapeDtypeS...  43.2 us
    unnamed x4, local copies, waits for them, and re-layouts  2.26 us

profile of v4, /device:TPU:0, one launch (start us, length us, event | category | flops | bytes accessed | tf_op | source)
XLA Modules:
  0.0 47.0 jit_solution(1069162449266365560)
XLA Ops:
  0.0 0.0 copy-start
  0.0 0.7 %convert_bitcast_fusion = bf16[1,128]{1,0:T(2,128)(2,1)S(1)} fusion(s32[128]{0:T(128)} %param.5), kind=kLoop, calls=%fused_computation.2 | loop fusion | flops 128 | bytes 768 | tf_op jit(solution)/shard_map/convert_element_type | solution.py:369
  0.7 0.1 pad.2.clone
  0.8 0.8 %maximum_maximum_fusion.pack = bf16[48,128]{1,0:T(8,128)(2,1)S(1)} fusion(bf16[1,128]{1,0:T(2,128)(2,1)S(1)} %convert_bitcast_fusion, bf16[40,128]{1,0:T(8,128)(2,1)} %bitcast.9, bf16[48]{0:T(256)(128)(2,1)S(1)} %pad.2.clone), kind=kLoop, calls=%fused_computation.1 | loop fusion | flops 36864 | bytes 22880 | tf_op jit(solution)/shard_map/concatenate | solution.py:366
  1.5 0.0 copy-done
  1.5 1.6 %copy.7 = bf16[128,4,8,128]{3,0,2,1:T(8,128)(2,1)S(1)} copy(bf16[128,4,8,128]{3,2,1,0:T(8,128)(2,1)} %param.4) | data formatting | bytes 2097152 | tf_op args[0]
  3.2 43.2 %shard_map.46 = f32[40,256]{1,0:T(8,128)S(1)} custom-call(bf16[4,8,128,128]{3,2,1,0:T(8,128)(2,1)S(1)} %bitcast.8, f32[4,8,128]{2,1,0:T(8,128)S(1)} %get-tuple-element.6.mask, f32[32,128]{1,0:T(8,128)S(1)} %get-tuple-element.5.mask_rows, bf16[48,128]{1,0:T(8,128)(2,1)S(1)} %maximum_maximum_fusion.pack), custom_call_target="tpu_custom_call" | custom-call | tf_op jit(solution)/shard_map/pallas_call | solution.py:374
  46.4 0.6 %copy.9 = f32[40,256]{1,0:T(8,128)} copy(f32[40,256]{1,0:T(8,128)S(1)} %shard_map.46) | data formatting | bytes 81920
  (2 shorter events, 0.0 us)
Async XLA Ops:
  0.0 1.5 %copy-start = (s32[4,8,128]{2,1,0:T(8,128)S(1)}, s32[4,8,128]{2,1,0:T(8,128)}, u32[]{:S(2)}) copy-start(s32[4,8,128]{2,1,0:T(8,128)} %param.7) | copy-start | bytes 49156

commit v5 on v4

--- a/solution.py
+++ b/solution.py
@@ -35,7 +35,7 @@
 def body(
     covars, x, mask, mask_rows, pack, out,
     low, high, mask_low, mask_high, mask_wide, p1, p2, smooth, recv, gathered, covs, flags_wide,
-    flags, flags_t, moments, tables, terms, all_terms,
+    flags, flags_t, moments, tables, centered, terms, all_terms,
     halo_send, halo_recv, mask_send, mask_recv, pack_send, pack_recv, fan_send, fan_recv,
     data_send, data_recv,
     own_sem, term_send, term_recv,
@@ -294,9 +294,18 @@
 
     @pl.loop(1, everyone)
     def _(step):
-        term_copy(step).start()
+        term_copy(everyone - step).start()
 
     all_terms[my_id] = terms[...]
+
+    pair = 2 if members % 2 == 0 else 1
+    for g in range(members // pair):
+        values = jnp.concatenate(
+            [recv[g * pair:(g + 1) * pair, r].reshape(pair * rows, width) for r in range(piece)],
+            axis=1,
+        ).astype(jnp.float32)
+        centered[g * pair * rows:(g + 1) * pair * rows] = values - voxel_mean
+
     all_others = pl.ds(0, everyone - 1)
     pltpu.make_async_copy(all_terms.at[all_others], all_terms.at[all_others], term_recv).wait()
     summed = jnp.sum(all_terms[...], axis=0)
@@ -320,16 +329,11 @@
     tables[:, :cells] = jnp.where(real, deviation * gamma_star, 0.0).astype(jnp.bfloat16)
     tables[:, cells:] = jnp.where(real, 1.0 / jnp.sqrt(delta_star), 0.0).astype(jnp.bfloat16)
 
-    pair = 2 if members % 2 == 0 else 1
     product = None
     for g in range(members // pair):
         span = slice(g * pair * rows, (g + 1) * pair * rows)
         picked = jnp.dot(flags[span], tables[...], preferred_element_type=jnp.float32)
-        values = jnp.concatenate(
-            [recv[g * pair:(g + 1) * pair, r].reshape(pair * rows, width) for r in range(piece)],
-            axis=1,
-        ).astype(jnp.float32)
-        adjusted = (values - voxel_mean - picked[:, :cells]) * picked[:, cells:] + voxel_mean
+        adjusted = (centered[span] - picked[:, :cells]) * picked[:, cells:] + voxel_mean
         partial = jnp.dot(
             covs[:, span], adjusted.astype(jnp.bfloat16), preferred_element_type=jnp.float32
         )
@@ -393,6 +397,7 @@
             pltpu.VMEM((CHUNKS, SITE_ROWS, members * rows // CHUNKS), bf16),
             pltpu.VMEM((SITE_ROWS, 2 * piece * width), f32),
             pltpu.VMEM((SITE_ROWS, 2 * piece * width), bf16),
+            pltpu.VMEM((members * rows, piece * width), f32),
             pltpu.VMEM((2, 128), f32),
             pltpu.VMEM((vox_count * members, 2, 128), f32),
             pltpu.SemaphoreType.DMA((2, CHUNKS)),

time: 47.3 us -> 48 us (1.015)
  Pallas kernels: 43.2 us -> 44 us
    pallas_call x1, Pallas kernels: 43.2 us -> 44 us  [per_device(): pl.pallas_call(functools.partial(body, covars), out_shape=jax.ShapeDtypeS...]
where the time goes in v5:
time: 48 us; the launch traced here: 47.8 us
  Pallas kernels  44 us (92%)
  local copies, waits for them, and re-layouts  2.34 us (5%)
  other arithmetic  1.45 us (3%)
    pallas_call x1, Pallas kernels, per_device(): pl.pallas_call(functools.partial(body, covars), out_shape=jax.ShapeDtypeS...  44 us
    unnamed x4, local copies, waits for them, and re-layouts  2.26 us

profile of v5, /device:TPU:0, one launch (start us, length us, event | category | flops | bytes accessed | tf_op | source)
XLA Modules:
  0.0 47.8 jit_solution(17490444593016321665)
XLA Ops:
  0.0 0.0 copy-start
  0.0 0.7 %convert_bitcast_fusion = bf16[1,128]{1,0:T(2,128)(2,1)S(1)} fusion(s32[128]{0:T(128)} %param.5), kind=kLoop, calls=%fused_computation.2 | loop fusion | flops 128 | bytes 768 | tf_op jit(solution)/shard_map/convert_element_type | solution.py:373
  0.7 0.1 pad.2.clone
  0.8 0.8 %maximum_maximum_fusion.pack = bf16[48,128]{1,0:T(8,128)(2,1)S(1)} fusion(bf16[1,128]{1,0:T(2,128)(2,1)S(1)} %convert_bitcast_fusion, bf16[40,128]{1,0:T(8,128)(2,1)} %bitcast.9, bf16[48]{0:T(256)(128)(2,1)S(1)} %pad.2.clone), kind=kLoop, calls=%fused_computation.1 | loop fusion | flops 36864 | bytes 22880 | tf_op jit(solution)/shard_map/concatenate | solution.py:370
  1.5 0.0 copy-done
  1.5 1.6 %copy.7 = bf16[128,4,8,128]{3,0,2,1:T(8,128)(2,1)S(1)} copy(bf16[128,4,8,128]{3,2,1,0:T(8,128)(2,1)} %param.4) | data formatting | bytes 2097152 | tf_op args[0]
  3.2 44.0 %shard_map.46 = f32[40,256]{1,0:T(8,128)S(1)} custom-call(bf16[4,8,128,128]{3,2,1,0:T(8,128)(2,1)S(1)} %bitcast.8, f32[4,8,128]{2,1,0:T(8,128)S(1)} %get-tuple-element.6.mask, f32[32,128]{1,0:T(8,128)S(1)} %get-tuple-element.5.mask_rows, bf16[48,128]{1,0:T(8,128)(2,1)S(1)} %maximum_maximum_fusion.pack), custom_call_target="tpu_custom_call" | custom-call | tf_op jit(solution)/shard_map/pallas_call | solution.py:378
  47.2 0.6 %copy.9 = f32[40,256]{1,0:T(8,128)} copy(f32[40,256]{1,0:T(8,128)S(1)} %shard_map.46) | data formatting | bytes 81920
  (2 shorter events, 0.0 us)
Async XLA Ops:
  0.0 1.5 %copy-start = (s32[4,8,128]{2,1,0:T(8,128)S(1)}, s32[4,8,128]{2,1,0:T(8,128)}, u32[]{:S(2)}) copy-start(s32[4,8,128]{2,1,0:T(8,128)} %param.7) | copy-start | bytes 49156

commit v6 on v4

--- a/solution.py
+++ b/solution.py
@@ -201,9 +201,12 @@
                 if target is not None:
                     stage = [functools.partial(lambda ref, k: ref[k], target, i) for i in range(count)]
 
-        @pl.loop(1, members)
-        def _(step):
-            send_piece(peer(members - step), c).start()
+        for away in sorted(range(nsubj), key=lambda d: -min(d, nsubj - d)):
+            line = lax.rem(subj + away, nsubj) * nsite
+
+            @pl.loop(0 if away else 1, nsite)
+            def _(step):
+                send_piece(line + lax.rem(site + step, nsite), c).start()
 
         @pl.when(c == 0)
         def _():

time: 47.3 us -> 47.9 us (1.013)
  Pallas kernels: 43.2 us -> 43.8 us
    pallas_call x1, Pallas kernels: 43.2 us -> 43.8 us  [per_device(): pl.pallas_call(functools.partial(body, covars), out_shape=jax.ShapeDtypeS...]
where the time goes in v6:
time: 47.9 us; the launch traced here: 47.6 us
  Pallas kernels  43.8 us (91%)
  local copies, waits for them, and re-layouts  2.34 us (5%)
  other arithmetic  1.45 us (3%)
    pallas_call x1, Pallas kernels, per_device(): pl.pallas_call(functools.partial(body, covars), out_shape=jax.ShapeDtypeS...  43.8 us
    unnamed x4, local copies, waits for them, and re-layouts  2.26 us

profile of v6, /device:TPU:0, one launch (start us, length us, event | category | flops | bytes accessed | tf_op | source)
XLA Modules:
  0.0 47.6 jit_solution(12844290066032286146)
XLA Ops:
  0.0 0.0 copy-start
  0.0 0.7 %convert_bitcast_fusion = bf16[1,128]{1,0:T(2,128)(2,1)S(1)} fusion(s32[128]{0:T(128)} %param.5), kind=kLoop, calls=%fused_computation.2 | loop fusion | flops 128 | bytes 768 | tf_op jit(solution)/shard_map/convert_element_type | solution.py:372
  0.7 0.1 pad.2.clone
  0.8 0.8 %maximum_maximum_fusion.pack = bf16[48,128]{1,0:T(8,128)(2,1)S(1)} fusion(bf16[1,128]{1,0:T(2,128)(2,1)S(1)} %convert_bitcast_fusion, bf16[40,128]{1,0:T(8,128)(2,1)} %bitcast.9, bf16[48]{0:T(256)(128)(2,1)S(1)} %pad.2.clone), kind=kLoop, calls=%fused_computation.1 | loop fusion | flops 36864 | bytes 22880 | tf_op jit(solution)/shard_map/concatenate | solution.py:369
  1.5 0.0 copy-done
  1.5 1.6 %copy.7 = bf16[128,4,8,128]{3,0,2,1:T(8,128)(2,1)S(1)} copy(bf16[128,4,8,128]{3,2,1,0:T(8,128)(2,1)} %param.4) | data formatting | bytes 2097152 | tf_op args[0]
  3.2 43.8 %shard_map.46 = f32[40,256]{1,0:T(8,128)S(1)} custom-call(bf16[4,8,128,128]{3,2,1,0:T(8,128)(2,1)S(1)} %bitcast.8, f32[4,8,128]{2,1,0:T(8,128)S(1)} %get-tuple-element.6.mask, f32[32,128]{1,0:T(8,128)S(1)} %get-tuple-element.5.mask_rows, bf16[48,128]{1,0:T(8,128)(2,1)S(1)} %maximum_maximum_fusion.pack), custom_call_target="tpu_custom_call" | custom-call | tf_op jit(solution)/shard_map/pallas_call | solution.py:377
  47.0 0.6 %copy.9 = f32[40,256]{1,0:T(8,128)} copy(f32[40,256]{1,0:T(8,128)S(1)} %shard_map.46) | data formatting | bytes 81920
  (2 shorter events, 0.0 us)
Async XLA Ops:
  0.0 1.5 %copy-start = (s32[4,8,128]{2,1,0:T(8,128)S(1)}, s32[4,8,128]{2,1,0:T(8,128)}, u32[]{:S(2)}) copy-start(s32[4,8,128]{2,1,0:T(8,128)} %param.7) | copy-start | bytes 49156
